TPU v7x, 512 devices: a whole 4x4x16 slice. The times are simulated.
512 devices in a mesh: stream: 32 (over x, y, core), cross: 16 (over z).
Axes of the slice: x: 4, y: 4, z: 16, core: 2. Of those that a mesh axis runs over, the one named last changes fastest.
Arguments:
- rhs: float32 [64, 5, 16384], P('stream', None, 'cross'), may hold values from -6 to 6
- diagonal: float32 [64, 16384], P('stream', 'cross'), may hold values from 1 to 10
- lower_transfer: float32 [64, 5, 5, 16384], P('stream', None, None, 'cross')
- upper_transfer: float32 [64, 5, 5, 16384], P('stream', None, None, 'cross')
- face_owner: int32 [16, 4], replicated, may hold values from 0 to 15, as said below
- face_start: int32 [16, 4], replicated, may hold values from 0 to 896, as said below
- face_count: int32 [16, 4], replicated, may hold values from 1 to 128, as said below
- face_flip: int32 [16, 4], replicated, may hold values from 0 to 1, as said below
- block_cells: int32 [16], replicated, may hold values from 512 to 1024
Outputs:
- solution: float32 [64, 5, 16384], P('stream', None, 'cross')
- residual: float32 [64, 5, 16384], P('stream', None, 'cross')
Inputs may be any that keep to these rules, and one draw needn't show every extreme that they name: Links pair up: if face_owner[j, l] = n then face_owner[n, l] = j and n != j. `face_start`: link l's face lies within cells l * 256 to (l + 1) * 256 - 1 of its block. `face_count`: both sides of a link have the same count. `face_flip`: both sides of a link have the same flag.
All inputs are finite; a program needn't handle non-finite values.
Results may differ from a plain program's by a relative error of at most 0.00018.
Values sent between devices are 32-bit elements; how exact they have to be, the bound alone decides.
No kernel may reach another device: no remote copies, remote signals or barrier semaphores. Data moves between devices by JAX's collectives and lax.ppermute only.
A program may use at most 64 MiB of HBM per device.

v0:
```python
import jax
import jax.numpy as jnp
from jax import lax
from jax.sharding import PartitionSpec as P

VARS = 5
LINKS = 4
FACE = 128
ITERS = 2


FACE_WEIGHT = 0.25


def shifted(shard, axis, by):
    size = lax.axis_size(axis)
    pairs = [(i, i + by) for i in range(size) if 0 <= i + by < size]
    return lax.ppermute(shard, axis, pairs)


def padded_2(shard, sides, width):
    for axis, dim in sides:
        size, length = (lax.axis_size(axis), shard.shape[dim])
        up = [(i, (i + 1) % size) for i in range(size - 1)]
        down = [(j, i) for i, j in up]
        last = lax.slice_in_dim(shard, length - width, length, axis=dim)
        first = lax.slice_in_dim(shard, 0, width, axis=dim)
        before = lax.ppermute(last, axis, up)
        after = lax.ppermute(first, axis, down)
        shard = jnp.concatenate([before, shard, after], axis=dim)
    return shard


def multiply(matrix, vector):
    return jnp.sum(matrix * vector[None, :, :], axis=1)


def compose(later, earlier):
    return jnp.sum(later[:, :, None, :] * earlier[None, :, :, :], axis=1)


def local_sweep(source, transfer, incoming, reverse):

    def advance(state, inputs):
        values, matrix = inputs
        state = values + multiply(matrix, state)
        return (state, state)

    _, result = lax.scan(advance, incoming, (source, transfer), reverse=reverse)
    return result


def local_map(transfer, identity, reverse):

    def advance(carried, matrix):
        return (compose(matrix, carried), None)

    result, _ = lax.scan(advance, identity, transfer, reverse=reverse)
    return result


def incoming_state(matrix, offset, reverse):
    blank = jnp.zeros_like(offset)
    turns = lax.axis_size("stream")
    if reverse:

        def relay_turn(turn, carried):
            arrived = shifted(carried[1], "stream", -1)
            return (arrived, multiply(matrix, arrived) + offset)

    else:

        def relay_turn(turn, carried):
            arrived = shifted(carried[1], "stream", 1)
            return (arrived, multiply(matrix, arrived) + offset)

    arrived, _ = lax.fori_loop(0, turns, relay_turn, (blank, offset))
    return arrived


def full_sweep(source, transfer, matrix, reverse):
    blank = jnp.zeros(source.shape[1:], jnp.float32)
    first_pass = local_sweep(source, transfer, blank, reverse)
    if reverse:
        offset = first_pass[0]
    else:
        offset = first_pass[-1]
    arrived = incoming_state(matrix, offset, reverse)
    return local_sweep(source, transfer, arrived, reverse)


def operate(
    field,
    diagonal,
    lower_transfer,
    upper_transfer,
    own_index,
    face_owner,
    face_start,
    face_count,
    face_flip,
):
    padded = padded_2(field, (("stream", 0),), 1)
    before = padded[:-2]
    after = padded[2:]
    along = jnp.sum(lower_transfer * before[:, None], axis=2) + jnp.sum(
        upper_transfer * after[:, None], axis=2
    )
    own_starts = face_start[own_index]
    published = jnp.stack(
        [lax.dynamic_slice_in_dim(field, own_starts[link], FACE, 2) for link in range(LINKS)]
    )
    flattened = published.reshape(LINKS, -1)
    wanted = face_owner[own_index] * LINKS + jnp.arange(LINKS, dtype=jnp.int32)
    piece = lax.all_gather(flattened, "cross", axis=0, tiled=True)
    row_index = jnp.arange(piece.shape[0], dtype=jnp.int32)
    selector = (wanted[:, None] == row_index[None, :]).astype(jnp.float32)
    received = jnp.dot(
        selector, piece, precision=lax.Precision.HIGHEST, preferred_element_type=jnp.float32
    )
    tile_sets = received.reshape(published.shape)
    positions = jnp.arange(FACE, dtype=jnp.int32)
    counts = face_count[own_index]
    flips = face_flip[own_index]
    picked = jnp.where(
        flips[:, None] == 1, counts[:, None] - 1 - positions[None, :], positions[None, :]
    )
    picked = jnp.clip(picked, 0, FACE - 1)
    picked = jnp.broadcast_to(picked[:, None, None, :], tile_sets.shape)
    oriented = jnp.take_along_axis(tile_sets, picked, axis=3)
    oriented = (
        oriented * (positions[None, :] < counts[:, None]).astype(jnp.float32)[:, None, None, :]
    )
    faces = jnp.zeros_like(field)
    for link in range(LINKS):
        current = lax.dynamic_slice_in_dim(faces, own_starts[link], FACE, 2)
        faces = lax.dynamic_update_slice_in_dim(
            faces, current + oriented[link], own_starts[link], 2
        )
    return diagonal[:, None, :] * (field - along - FACE_WEIGHT * faces)


def local(
    rhs,
    diagonal,
    lower_transfer,
    upper_transfer,
    face_owner,
    face_start,
    face_count,
    face_flip,
    block_cells,
):
    own_index = lax.axis_index("cross")
    cells = rhs.shape[2]
    live_mask = (jnp.arange(cells, dtype=jnp.int32) < block_cells[own_index]).astype(jnp.float32)
    live_source = rhs * live_mask[None, None, :]
    identity = jnp.broadcast_to(jnp.eye(VARS, dtype=jnp.float32)[:, :, None], (VARS, VARS, cells))
    lower_matrix = local_map(lower_transfer, identity, False)
    upper_matrix = local_map(upper_transfer, identity, True)
    solution = jnp.zeros_like(rhs)
    residual = live_source
    for iteration in range(ITERS):
        lowered = full_sweep(residual / diagonal[:, None, :], lower_transfer, lower_matrix, False)
        delta = full_sweep(lowered, upper_transfer, upper_matrix, True)
        solution = solution + delta
        residual = live_source - operate(
            solution,
            diagonal,
            lower_transfer,
            upper_transfer,
            own_index,
            face_owner,
            face_start,
            face_count,
            face_flip,
        )
    return (solution, residual)


def solution(mesh):
    return jax.shard_map(
        local,
        mesh=mesh,
        in_specs=(
            P("stream", None, "cross"),
            P("stream", "cross"),
            P("stream", None, None, "cross"),
            P("stream", None, None, "cross"),
            P(),
            P(),
            P(),
            P(),
            P(),
        ),
        out_specs=(P("stream", None, "cross"), P("stream", None, "cross")),
        check_vma=False,
    )
```

profile of v0, /device:TPU:6, one launch (start us, length us, event | category | flops | bytes accessed | tf_op | source)
XLA Modules:
  0.0 1206.2 jit_solution(16427889050841771946)
XLA Ops:
  4.8 254.3 %while.189 = (s32[]{:T(128)}, f32[5,1024]{1,0:T(8,128)}, f32[5,1024]{1,0:T(8,128)S(1)}, f32[5,5,1024]{2,1,0:T(8,128)S(1)}, f32[5,1024]{1,0:T(8,128)S(1)}, /*index=5*/s32[]{:T(128)}) while((s32[]{:T(128)}, f32[5,1024]{1,0:T(8,128)}, f32[5,1024]{1,0:T(8,128)S(1)}, f32[5,5,1024]{2,1,0:T(8,128)S(1)}, f32[5,1024]{1,0:T(8,128)S(1)}, ...), condition=%wide.region_8.9_spmd, body=%wide.region_6.8_spmd.sunk | while | flops 51202 | bytes 368777 | solution.py:77
  263.5 250.5 %while.192 = (s32[]{:T(128)}, f32[5,1024]{1,0:T(8,128)}, f32[5,1024]{1,0:T(8,128)S(1)}, f32[5,5,1024]{2,1,0:T(8,128)S(1)}, f32[5,1024]{1,0:T(8,128)S(1)}, /*index=5*/s32[]{:T(128)}) while((s32[]{:T(128)}, f32[5,1024]{1,0:T(8,128)}, f32[5,1024]{1,0:T(8,128)S(1)}, f32[5,5,1024]{2,1,0:T(8,128)S(1)}, f32[5,1024]{1,0:T(8,128)S(1)}, ...), condition=%wide.region_20.21_spmd, body=%wide.region_18.20_spmd.sunk | while | flops 51202 | bytes 368777 | solution.py:77
  267.6 5.7 collective-permute-start.1
  275.6 5.7 collective-permute-start.1
  283.5 5.7 collective-permute-start.1
  307.4 5.7 collective-permute-start.1
  315.3 5.7 collective-permute-start.1
  323.3 5.7 collective-permute-start.1
  331.2 5.7 collective-permute-start.1
  339.1 5.7 collective-permute-start.1
  347.1 5.7 collective-permute-start.1
  355.0 5.7 collective-permute-start.1
  386.8 5.7 collective-permute-start.1
  394.8 5.7 collective-permute-start.1
  402.7 5.7 collective-permute-start.1
  410.7 5.7 collective-permute-start.1
  518.9 5.8 collective-permute-start.5
  533.7 37.2 %all-gather = f32[16,4,1280]{2,1,0:T(4,128)S(1)} all-gather(f32[1,4,1280]{2,1,0:T(4,128)S(1)} %maximum_bitcast_fusion), channel_id=1, replica_groups=mesh['stream'=32,'cross'=16] {'cross'}, dimensions={0}, use_global_device_ids=true | all-gather | bytes 348160 | tf_op jit(solution)/shard_map/all_gather | solution.py:115
  572.1 38.4 %gather_fusion = f32[5120]{0:T(1024)S(1)} fusion(f32[4,2,5,128]{3,2,1,0:T(8,128)S(1)} %reshape.195, s32[5120]{0:T(1024)S(1)} %reshape.225), kind=kCustom, calls=%fused_computation.clone | custom fusion | bytes 122880 | tf_op jit(solution)/shard_map/jit(take_along_axis)/gather | solution.py:130
  615.0 254.3 %while.194 = (s32[]{:T(128)}, f32[5,1024]{1,0:T(8,128)}, f32[5,1024]{1,0:T(8,128)S(1)}, f32[5,5,1024]{2,1,0:T(8,128)S(1)}, f32[5,1024]{1,0:T(8,128)S(1)}, /*index=5*/s32[]{:T(128)}) while((s32[]{:T(128)}, f32[5,1024]{1,0:T(8,128)}, f32[5,1024]{1,0:T(8,128)S(1)}, f32[5,5,1024]{2,1,0:T(8,128)S(1)}, f32[5,1024]{1,0:T(8,128)S(1)}, ...), condition=%wide.region_31.33_spmd, body=%wide.region_29.32_spmd.sunk | while | flops 51202 | bytes 368777 | solution.py:77
  873.1 250.5 %while.196 = (s32[]{:T(128)}, f32[5,1024]{1,0:T(8,128)}, f32[5,1024]{1,0:T(8,128)S(1)}, f32[5,5,1024]{2,1,0:T(8,128)S(1)}, f32[5,1024]{1,0:T(8,128)S(1)}, /*index=5*/s32[]{:T(128)}) while((s32[]{:T(128)}, f32[5,1024]{1,0:T(8,128)}, f32[5,1024]{1,0:T(8,128)S(1)}, f32[5,5,1024]{2,1,0:T(8,128)S(1)}, f32[5,1024]{1,0:T(8,128)S(1)}, ...), condition=%wide.region_40.42_spmd, body=%wide.region_38.41_spmd.sunk | while | flops 51202 | bytes 368777 | solution.py:77
  1129.0 5.8 collective-permute-start.7
  1134.9 29.0 %all-gather.1 = f32[16,4,1280]{2,1,0:T(4,128)S(1)} all-gather(f32[1,4,1280]{2,1,0:T(4,128)S(1)} %maximum_bitcast_fusion.1), channel_id=1, replica_groups=mesh['stream'=32,'cross'=16] {'cross'}, dimensions={0}, use_global_device_ids=true | all-gather | bytes 348160 | tf_op jit(solution)/shard_map/all_gather | solution.py:115
  1164.3 38.4 %gather_fusion.1 = f32[5120]{0:T(1024)S(1)} fusion(f32[4,2,5,128]{3,2,1,0:T(8,128)S(1)} %reshape.196, s32[5120]{0:T(1024)S(1)} %reshape.225), kind=kCustom, calls=%fused_computation.1.clone | custom fusion | bytes 122880 | tf_op jit(solution)/shard_map/jit(take_along_axis)/gather | solution.py:130
  (962 shorter events, 972.6 us)
Async XLA Ops:
  267.6 7.3 collective-permute-start.1
  275.6 7.3 collective-permute-start.1
  283.5 7.3 collective-permute-start.1
  291.5 7.3 collective-permute-start.1
  299.4 7.3 collective-permute-start.1
  307.4 7.3 collective-permute-start.1
  315.3 7.3 collective-permute-start.1
  323.3 7.3 collective-permute-start.1
  331.2 7.3 collective-permute-start.1
  339.1 7.3 collective-permute-start.1
  347.1 7.3 collective-permute-start.1
  355.0 7.3 collective-permute-start.1
  370.9 7.3 collective-permute-start.1
  378.9 7.3 collective-permute-start.1
  386.8 7.3 collective-permute-start.1
  394.8 7.3 collective-permute-start.1
  402.7 7.3 collective-permute-start.1
  410.7 7.3 collective-permute-start.1
  418.6 7.3 collective-permute-start.1
  426.6 7.3 collective-permute-start.1
  517.0 96.1 %collective-permute-start.4 = (f32[1,5,1024]{2,1,0:T(8,128)S(1)}, f32[1,5,1024]{2,1,0:T(8,128)S(1)}, u32[]{:S(2)}, u32[]{:S(2)}) collective-permute-start(f32[1,5,1024]{2,1,0:T(8,128)S(1)} %get-tuple-element.1110), channel_id=1, source_target_pairs={{0,16},{16,32},{32,48},{48,64},{64,80},{80,96},{96,112},{112,128},... | collective-permute-start | bytes 61448 | tf_op jit(solution)/shard_map/ppermute | solution.py:28
  518.9 94.2 %collective-permute-start.5 = (f32[1,5,1024]{2,1,0:T(8,128)S(1)}, f32[1,5,1024]{2,1,0:T(8,128)S(1)}, u32[]{:S(2)}, u32[]{:S(2)}) collective-permute-start(f32[1,5,1024]{2,1,0:T(8,128)S(1)} %get-tuple-element.1109), channel_id=1, source_target_pairs={{16,0},{32,16},{48,32},{64,48},{80,64},{96,80},{112,96},{128,112},... | collective-permute-start | bytes 61448 | tf_op jit(solution)/shard_map/ppermute | solution.py:29
  1127.1 78.1 %collective-permute-start.6 = (f32[1,5,1024]{2,0,1:T(1,128)S(1)}, f32[1,5,1024]{2,0,1:T(1,128)S(1)}, u32[]{:S(2)}, u32[]{:S(2)}) collective-permute-start(f32[1,5,1024]{2,0,1:T(1,128)S(1)} %get-tuple-element.1118), channel_id=1, source_target_pairs={{0,16},{16,32},{32,48},{48,64},{64,80},{80,96},{96,112},{112,128},... | collective-permute-start | bytes 61448 | tf_op jit(solution)/shard_map/ppermute | solution.py:28
  1129.0 76.2 %collective-permute-start.7 = (f32[1,5,1024]{2,0,1:T(1,128)S(1)}, f32[1,5,1024]{2,0,1:T(1,128)S(1)}, u32[]{:S(2)}, u32[]{:S(2)}) collective-permute-start(f32[1,5,1024]{2,0,1:T(1,128)S(1)} %get-tuple-element.1117), channel_id=1, source_target_pairs={{16,0},{32,16},{48,32},{64,48},{80,64},{96,80},{112,96},{128,112},... | collective-permute-start | bytes 61448 | tf_op jit(solution)/shard_map/ppermute | solution.py:29
  (245 other events, 987.2 us)
where the time goes:
time: 1210 us
  starting transfers between devices  498 us (41%)
  waiting for transfers between devices  447 us (37%)
  local copies, waits for them, and re-layouts  157 us (13%)
  blocking collectives  66.2 us (5%)
  other arithmetic  24.8 us (2%)
    ppermute x128, starting transfers between devices, shifted(): return lax.ppermute(shard, axis, pairs)  482 us
    ppermute x128, waiting for transfers between devices, shifted(): return lax.ppermute(shard, axis, pairs)  447 us
    gather x6, local copies, waits for them, and re-layouts, operate(): oriented = jnp.take_along_axis(tile_sets, picked, axis=3)  76.9 us
    while x260, local copies, waits for them, and re-layouts  69.1 us
    all_gather x2, blocking collectives, operate(): piece = lax.all_gather(flattened, 'cross', axis=0, tiled=True)  66.2 us
  transfers between devices with their start and end apart: 132, of which 128 were waited for; matrix products, arithmetic and copies ran while one was open for 7% of the time, Pallas kernels for 0%

commit v1 on v0

v1 whole, which is shorter than its diff:
```python
import functools

import jax
import jax.numpy as jnp
from jax import lax
from jax.experimental import pallas as pl
from jax.experimental.pallas import tpu as pltpu
from jax.sharding import PartitionSpec as P

VARS = 5
CELLS = 1024
LINKS = 4
WINDOW = CELLS // LINKS
STREAM = 32
CROSS = 16
PLANES = 2
CHUNKS = 8
GROUPS = 4
LANES = 128
FACE_WEIGHT = 0.25

LOWER = 0
UPPER = 25
SOURCE = 50
ROWS = 110

F32 = jnp.float32
BF16 = jnp.bfloat16
SMEM = pl.BlockSpec(memory_space=pltpu.SMEM)
VMEM = pl.BlockSpec(memory_space=pltpu.VMEM)
PARAMS = pltpu.CompilerParams(vmem_limit_bytes=24 * 1024 * 1024)


def cost(flops, moved):
    return pl.CostEstimate(flops=flops, bytes_accessed=moved, transcendentals=0)


def thirds(x):
    high = x.astype(BF16)
    rest = x - high.astype(F32)
    middle = rest.astype(BF16)
    low = (rest - middle.astype(F32)).astype(BF16)
    return high, middle, low


def slot_map(own, link, owner_ref, start_ref, count_ref, flip_ref):
    owner = owner_ref[link, own]
    count = count_ref[link, own]
    turned = jnp.logical_and(flip_ref[link, own] == 1, own > owner)
    bound = jnp.where(turned, count, 0)
    offset = start_ref[link, own] - link * WINDOW
    cell = lax.broadcasted_iota(jnp.int32, (1, WINDOW), 1)
    place = (cell - offset) & (WINDOW - 1)
    place = jnp.where(place < bound, count - 1 - place, place)
    rest = place & 127
    slot = ((rest >> 4) << 5) + (rest & 15) + ((place >> 7) << 4)
    rows = lax.broadcasted_iota(jnp.int32, (WINDOW, WINDOW), 0)
    return jnp.where(rows == slot, 1.0, 0.0).astype(BF16)


def pack_kernel(
    owner_ref, start_ref, count_ref, flip_ref, live_ref,
    rhs_ref, diagonal_ref, lower_ref, upper_ref, out_ref, rows_ref,
):
    own = lax.axis_index("cross")
    cell = lax.broadcasted_iota(jnp.int32, (PLANES, CELLS), 1)
    live = cell < live_ref[own]
    for a in range(VARS):
        for b in range(VARS):
            at = VARS * a + b
            rows_ref[pl.ds(2 * (LOWER + at), 2), :] = lower_ref[a, b]
            rows_ref[pl.ds(2 * (UPPER + at), 2), :] = upper_ref[a, b]
        source = jnp.where(live, rhs_ref[a], 0.0) / diagonal_ref[...]
        rows_ref[pl.ds(2 * (SOURCE + a), 2), :] = source
    rows_ref[pl.ds(ROWS, LANES - ROWS), :] = jnp.zeros((LANES - ROWS, CELLS), F32)
    for link in range(LINKS):
        onehot = slot_map(own, link, owner_ref, start_ref, count_ref, flip_ref)
        parts = thirds(rows_ref[:, link * WINDOW:(link + 1) * WINDOW])
        high, middle, low = [
            lax.dot_general(onehot, part, (((1,), (1,)), ((), ())), preferred_element_type=F32)
            for part in parts
        ]
        out_ref[link * WINDOW:(link + 1) * WINDOW, :] = (low + middle) + high


def entry(system_ref, k, p, at):
    row = 2 * at + p
    return system_ref[k, row:row + 1, :]


def product(system_ref, k, p, at, state):
    out = []
    for a in range(VARS):
        terms = [
            entry(system_ref, k, p, at + VARS * a + b) * state[b] for b in range(VARS)
        ]
        out.append((terms[0] + terms[1]) + (terms[2] + terms[3]) + terms[4])
    return out


def get_rows(ref, k, p):
    return [ref[k, 8 * p + a:8 * p + a + 1, :] for a in range(VARS)]


def put_rows(ref, k, p, rows):
    for a in range(VARS):
        ref[k, 8 * p + a:8 * p + a + 1, :] = rows[a]


def turn(state, by):
    return tuple(pltpu.roll(x, by, 1) for x in state)


def lower_sweep(step):
    state = tuple(jnp.zeros((1, LANES), F32) for _ in range(VARS))
    for group in range(GROUPS):
        if group:
            state = turn(state, 32)
        state = lax.fori_loop(0, CHUNKS, functools.partial(step, group), state, unroll=True)


def upper_sweep(step):
    state = tuple(jnp.zeros((1, LANES), F32) for _ in range(VARS))
    for group in reversed(range(GROUPS)):
        if group < GROUPS - 1:
            state = turn(state, 96)
        state = lax.fori_loop(
            0, CHUNKS, lambda i, x: step(group, CHUNKS - 1 - i, x), state, unroll=True
        )


def merged(ref):
    shape = (CHUNKS * 16, LANES)
    lane = lax.broadcasted_iota(jnp.int32, shape, 1) >> 5
    row = lax.broadcasted_iota(jnp.int32, shape, 0) & 7
    parts = [ref[group].reshape(shape) for group in range(GROUPS)]
    out = jnp.where(lane == 0, parts[0], jnp.where(lane == 1, parts[1], jnp.where(lane == 2, parts[2], parts[3])))
    return jnp.where(row < VARS, out, 0.0)


def publish(field, send_ref):
    turned = field.T
    for group in range(GROUPS):
        send_ref[pl.ds(group, 16, stride=GROUPS), :] = turned[32 * group:32 * group + 16]


def receive(face_ref):
    parts = []
    for group in range(GROUPS):
        parts.append(face_ref[pl.ds(group, 16, stride=GROUPS), :])
        parts.append(jnp.zeros((16, LANES), F32))
    return FACE_WEIGHT * jnp.concatenate(parts, axis=0).T


def upper_pass(system_ref, lowered_ref, coupled_ref, delta_ref):
    def upper(group, k, state):
        for p in reversed(range(PLANES)):
            coupled = product(system_ref, k, p, UPPER, state)
            put_rows(coupled_ref.at[group], k, p, coupled)
            lowered = get_rows(lowered_ref.at[group], k, p)
            state = tuple(w + e for w, e in zip(lowered, coupled))
            put_rows(delta_ref.at[group], k, p, state)
        return state

    upper_sweep(upper)


def first_kernel(in_ref, system_ref, coupled_out, delta_out, send_ref, lowered_ref, coupled_ref, delta_ref):
    for k in range(CHUNKS):
        block = jnp.concatenate([in_ref[CHUNKS * g + k] for g in range(GROUPS)], axis=0)
        system_ref[k] = block.T

    def lower(group, k, state):
        for p in range(PLANES):
            along = product(system_ref, k, p, LOWER, state)
            state = tuple(entry(system_ref, k, p, SOURCE + a) + along[a] for a in range(VARS))
            put_rows(lowered_ref.at[group], k, p, state)
        return state

    lower_sweep(lower)
    upper_pass(system_ref, lowered_ref, coupled_ref, delta_ref)
    coupled_out[...] = merged(coupled_ref).reshape(coupled_out.shape)
    delta = merged(delta_ref)
    delta_out[...] = delta
    publish(delta, send_ref)


def swap_kernel(owner_ref, count_ref, in_ref, out_ref):
    position = lax.axis_index("stream")
    link = position >> 3
    slot = ((position & 7) << 4) + lax.axis_index("cross")
    for block in range(CROSS):
        tile = in_ref[owner_ref[link, block]]
        keep = jnp.full(tile.shape, count_ref[link, block], jnp.int32) > slot
        out_ref[block] = jnp.where(keep, tile, 0.0)


def second_kernel(
    system_ref, coupled_in, delta_in, face_ref,
    solution_ref, along_ref, send_ref,
    faces_ref, lowered_ref, coupled_ref, delta_ref, last_ref,
):
    faces_ref[...] = receive(face_ref).reshape(faces_ref.shape)

    def lower(group, k, state):
        for p in range(PLANES):
            along = product(system_ref, k, p, LOWER, state)
            faces = get_rows(faces_ref, k, p)
            lowered = [f + x for f, x in zip(faces, along)]
            put_rows(lowered_ref.at[group], k, p, lowered)
            before = get_rows(coupled_in, k, p)
            state = tuple(w + e for w, e in zip(lowered, before))
        return state

    lower_sweep(lower)
    upper_pass(system_ref, lowered_ref, coupled_ref, delta_ref)
    delta = merged(delta_ref)
    publish(delta, send_ref)
    solution_ref[...] = delta_in[...] + delta
    last_ref[...] = merged(coupled_ref).reshape(last_ref.shape)
    lane = lax.broadcasted_iota(jnp.int32, (1, LANES), 1)
    for k in range(CHUNKS):
        if k:
            before = get_rows(last_ref, k - 1, 1)
        else:
            before = [
                jnp.where(lane < 32, 0.0, x) for x in turn(get_rows(last_ref, CHUNKS - 1, 1), 32)
            ]
        put_rows(along_ref, k, 0, product(system_ref, k, 0, LOWER, before))
        before = get_rows(last_ref, k, 0)
        put_rows(along_ref, k, 1, product(system_ref, k, 1, LOWER, before))


def regroup(parts):
    lane = lax.broadcasted_iota(jnp.int32, parts[0].shape, 1)
    first_half = lane < 64
    even = (lane & 32) == 0
    half = [None] * 4
    for i in range(2):
        x, y = parts[i], parts[i + 2]
        half[i] = jnp.where(first_half, x, pltpu.roll(y, 64, 1))
        half[i + 2] = jnp.where(first_half, pltpu.roll(x, 64, 1), y)
    out = [None] * 4
    for i in (0, 2):
        x, y = half[i], half[i + 1]
        out[i] = jnp.where(even, x, pltpu.roll(y, 32, 1))
        out[i + 1] = jnp.where(even, pltpu.roll(x, 96, 1), y)
    return out


def last_kernel(solution_ref, along_ref, face_ref, out_ref, residual_ref):
    residual_ref[...] = along_ref[...] + receive(face_ref).reshape(residual_ref.shape)
    for k in range(CHUNKS):
        tiles = [solution_ref[16 * k + 8 * p:16 * k + 8 * p + 8, :] for p in range(PLANES)]
        tiles += [residual_ref[k, 8 * p:8 * p + 8, :] for p in range(PLANES)]
        for group, tile in enumerate(regroup(tiles)):
            out_ref[CHUNKS * group + k] = tile


def unpack_kernel(
    owner_ref, start_ref, count_ref, flip_ref, diagonal_ref, in_ref, solution_ref, residual_ref, rows_ref
):
    own = lax.axis_index("cross")
    for column in range(8):
        tiles = regroup([in_ref[4 * column + e] for e in range(4)])
        for g, tile in enumerate(tiles):
            rows_ref[8 * g:8 * g + 8, LANES * column:LANES * (column + 1)] = tile
    for link in range(LINKS):
        window = slice(link * WINDOW, (link + 1) * WINDOW)
        onehot = slot_map(own, link, owner_ref, start_ref, count_ref, flip_ref)
        high, middle, low = [
            jnp.dot(part, onehot, preferred_element_type=F32) for part in thirds(rows_ref[:, window])
        ]
        cells = (low + middle) + high
        for p in range(PLANES):
            residual = cells[16 + 8 * p:16 + 8 * p + VARS] * diagonal_ref[p:p + 1, window]
            for a in range(VARS):
                solution_ref[a, p:p + 1, window] = cells[8 * p + a:8 * p + a + 1]
                residual_ref[a, p:p + 1, window] = residual[a:a + 1]


def shape(*dims):
    return jax.ShapeDtypeStruct(dims, F32)


def exchange(send, face_owner, face_count):
    arrived = lax.all_to_all(send.reshape(CROSS, GROUPS, LANES), "cross", 0, 0, tiled=True)
    swapped = pl.pallas_call(
        swap_kernel,
        out_shape=shape(CROSS, GROUPS, LANES),
        in_specs=[SMEM, SMEM, VMEM],
        out_specs=VMEM,
        name="swap_faces",
    )(face_owner, face_count, arrived)
    back = lax.all_to_all(swapped, "cross", 0, 0, tiled=True)
    return back.reshape(CROSS * GROUPS, LANES)


def local(
    rhs,
    diagonal,
    lower_transfer,
    upper_transfer,
    face_owner,
    face_start,
    face_count,
    face_flip,
    block_cells,
):
    face_owner, face_count = face_owner.T, face_count.T
    links = (face_owner, face_start.T, face_count, face_flip.T)
    packed = pl.pallas_call(
        pack_kernel,
        out_shape=shape(CELLS, LANES),
        in_specs=[SMEM] * 5 + [VMEM] * 4,
        out_specs=VMEM,
        scratch_shapes=[pltpu.VMEM((LANES, CELLS), F32)],
        compiler_params=PARAMS,
        name="pack_cells",
    )(
        *links,
        block_cells,
        rhs.transpose(1, 0, 2),
        diagonal,
        lower_transfer.transpose(1, 2, 0, 3),
        upper_transfer.transpose(1, 2, 0, 3),
    )
    arrived = lax.all_to_all(packed.reshape(STREAM, 32, LANES), "stream", 0, 0, tiled=True)

    passes = pltpu.VMEM((GROUPS, CHUNKS, 16, LANES), F32)
    system, coupled, delta, send = pl.pallas_call(
        first_kernel,
        out_shape=[
            shape(CHUNKS, LANES, LANES), shape(CHUNKS, 16, LANES), shape(LANES, LANES), shape(64, LANES)
        ],
        in_specs=[VMEM],
        out_specs=[VMEM] * 4,
        scratch_shapes=[passes] * 3,
        compiler_params=PARAMS,
        name="first_sweeps",
    )(arrived)
    faces = exchange(send, face_owner, face_count)
    total, along, send = pl.pallas_call(
        second_kernel,
        out_shape=[shape(LANES, LANES), shape(CHUNKS, 16, LANES), shape(64, LANES)],
        in_specs=[VMEM] * 4,
        out_specs=[VMEM] * 3,
        scratch_shapes=[pltpu.VMEM((CHUNKS, 16, LANES), F32)] + [passes] * 3
        + [pltpu.VMEM((CHUNKS, 16, LANES), F32)],
        compiler_params=PARAMS,
        name="second_sweeps",
    )(system, coupled, delta, faces)
    faces = exchange(send, face_owner, face_count)
    results = pl.pallas_call(
        last_kernel,
        out_shape=shape(STREAM, 8, LANES),
        in_specs=[VMEM] * 3,
        out_specs=VMEM,
        scratch_shapes=[pltpu.VMEM((CHUNKS, 16, LANES), F32)],
        compiler_params=PARAMS,
        name="pack_results",
    )(total, along, faces)
    returned = lax.all_to_all(results, "stream", 0, 0, tiled=True)
    results = pl.pallas_call(
        unpack_kernel,
        out_shape=[shape(VARS, PLANES, CELLS)] * 2,
        in_specs=[SMEM] * 4 + [VMEM] * 2,
        out_specs=[VMEM] * 2,
        scratch_shapes=[pltpu.VMEM((32, CELLS), F32)],
        compiler_params=PARAMS,
        name="unpack_cells",
    )(*links, diagonal, returned)
    return tuple(x.transpose(1, 0, 2) for x in results)


def solution(mesh):
    return jax.shard_map(
        local,
        mesh=mesh,
        in_specs=(
            P("stream", None, "cross"),
            P("stream", "cross"),
            P("stream", None, None, "cross"),
            P("stream", None, None, "cross"),
            P(),
            P(),
            P(),
            P(),
            P(),
        ),
        out_specs=(P("stream", None, "cross"), P("stream", None, "cross")),
        check_vma=False,
    )
```

time: 1210 us -> 122 us (0.10)
  the two profiles are of different devices: /device:TPU:6 before, /device:TPU:1 now
where the time goes in v1:
time: 122 us
  blocking collectives  107 us (88%)
  Pallas kernels  9.38 us (8%)
  local copies, waits for them, and re-layouts  4.71 us (4%)
    all_to_all x2, blocking collectives, exchange(): lax.all_to_all(send.reshape(CROSS, GROUPS, LANES), 'cross', 0, 0, tiled=T...  39.6 us
    all_to_all x2, blocking collectives, exchange(): back = lax.all_to_all(swapped, 'cross', 0, 0, tiled=True)  29.7 us
    all_to_all x1, blocking collectives, local(): lax.all_to_all(packed.reshape(STREAM, 32, LANES), 'stream', 0, 0, tiled=T...  21.3 us
    all_to_all x1, blocking collectives, local(): returned = lax.all_to_all(results, 'stream', 0, 0, tiled=True)  16.3 us
    unnamed x26, local copies, waits for them, and re-layouts  4.71 us
    pallas_call x2, Pallas kernels, exchange(): pl.pallas_call(swap_kernel, out_shape=shape(CROSS, GROUPS, LANES), in_spe...  2.83 us

profile of v1, /device:TPU:1, one launch (start us, length us, event | category | flops | bytes accessed | tf_op | source)
XLA Modules:
  0.0 121.7 jit_solution(1345153270313416011)
XLA Ops:
  0.6 0.0 copy-start.6
  0.7 0.0 copy-start.4
  0.7 0.7 copy-done.3
  1.3 0.0 copy-done.4
  1.4 0.9 copy-done
  2.3 0.9 copy-done.1
  3.2 0.8 copy-done.2
  4.0 0.7 copy-done.8
  4.7 0.7 copy-done.10
  5.4 1.4 %pack_cells.1 = f32[1024,128]{1,0:T(8,128)S(1)} custom-call(s32[4,16]{1,0:T(4,128)S(1)} %bitcast.22, s32[4,16]{1,0:T(4,128)S(1)} %bitcast.30, s32[4,16]{1,0:T(4,128)S(1)} %bitcast.26, s32[4,16]{1,0:T(4,128)S(1)} %bitcast.32, s32[16]{0:T(128)S(1)} %copy-done.12, f32[5,2,1024]{2,1,0:T(2,128)S(1)} %bitcast.19, f32[2,1024]{1,0:T(2,128)S(1)} %copy-done.3, ...), custom_call_target="tpu_custom_call" | custom-call | tf_op jit(solution)/shard_map/pack_cells/pallas_call | solution.py:312
  6.7 21.3 %all_to_all.30.in_ref = f32[32,32,128]{2,1,0:T(8,128)S(1)} all-to-all(f32[32,32,128]{2,1,0:T(8,128)S(1)} %bitcast.14), channel_id=1, replica_groups=mesh['stream'=32,'cross'=16] {'stream'}, dimensions={0} | all-to-all | bytes 1048576 | tf_op jit(solution)/shard_map/all_to_all | solution.py:328
  28.0 1.6 %first_sweeps.1 = (f32[8,128,128]{2,1,0:T(8,128)S(1)}, f32[8,16,128]{2,1,0:T(8,128)S(1)}, f32[128,128]{1,0:T(8,128)S(1)}, f32[64,128]{1,0:T(8,128)S(1)}) custom-call(f32[32,32,128]{2,1,0:T(8,128)S(1)} %all_to_all.30.in_ref), custom_call_target="tpu_custom_call" | custom-call | tf_op jit(solution)/shard_map/first_sweeps/pallas_call | solution.py:331
  29.5 25.1 %all_to_all.31.in_ref = f32[16,4,128]{2,1,0:T(4,128)} all-to-all(f32[16,4,128]{2,1,0:T(4,128)S(1)} %bitcast.29), channel_id=1, replica_groups=mesh['stream'=32,'cross'=16] {'cross'}, dimensions={0} | all-to-all | bytes 65536 | tf_op jit(solution)/shard_map/all_to_all | solution.py:287
  54.6 1.4 %swap_faces.2 = f32[16,4,128]{2,1,0:T(4,128)} custom-call(s32[4,16]{1,0:T(4,128)} %bitcast.20, s32[4,16]{1,0:T(4,128)} %bitcast.24, f32[16,4,128]{2,1,0:T(4,128)} %all_to_all.31.in_ref), custom_call_target="tpu_custom_call" | custom-call | tf_op jit(solution)/shard_map/swap_faces/pallas_call | solution.py:288
  56.1 14.9 %all_to_all.32 = f32[16,4,128]{2,1,0:T(4,128)S(1)} all-to-all(f32[16,4,128]{2,1,0:T(4,128)} %swap_faces.2), channel_id=1, replica_groups=mesh['stream'=32,'cross'=16] {'cross'}, dimensions={0} | all-to-all | bytes 65536 | tf_op jit(solution)/shard_map/all_to_all | solution.py:295
  71.0 1.6 %second_sweeps.1 = (f32[128,128]{1,0:T(8,128)S(1)}, f32[8,16,128]{2,1,0:T(8,128)S(1)}, f32[64,128]{1,0:T(8,128)S(1)}) custom-call(f32[8,128,128]{2,1,0:T(8,128)S(1)} %get-tuple-element.11.system_ref, f32[8,16,128]{2,1,0:T(8,128)S(1)} %get-tuple-element.12.coupled_in, f32[128,128]{1,0:T(8,128)S(1)} %get-tuple-element.13.delta_in, f32[64,128]{1,0:T(8,128)S(1)} %bitcast.18), custom_call_target="tpu_custom_call" | custom-call | tf_op jit(solution)/shard_map/second_sweeps/pallas_call | solution.py:343
  72.6 14.5 %all_to_all.33.in_ref = f32[16,4,128]{2,1,0:T(4,128)} all-to-all(f32[16,4,128]{2,1,0:T(4,128)S(1)} %bitcast.28), channel_id=1, replica_groups=mesh['stream'=32,'cross'=16] {'cross'}, dimensions={0} | all-to-all | bytes 65536 | tf_op jit(solution)/shard_map/all_to_all | solution.py:287
  87.1 1.4 %swap_faces.3 = f32[16,4,128]{2,1,0:T(4,128)} custom-call(s32[4,16]{1,0:T(4,128)} %bitcast.21, s32[4,16]{1,0:T(4,128)} %bitcast.25, f32[16,4,128]{2,1,0:T(4,128)} %all_to_all.33.in_ref), custom_call_target="tpu_custom_call" | custom-call | tf_op jit(solution)/shard_map/swap_faces/pallas_call | solution.py:288
  88.5 14.8 %all_to_all.34 = f32[16,4,128]{2,1,0:T(4,128)S(1)} all-to-all(f32[16,4,128]{2,1,0:T(4,128)} %swap_faces.3), channel_id=1, replica_groups=mesh['stream'=32,'cross'=16] {'cross'}, dimensions={0} | all-to-all | bytes 65536 | tf_op jit(solution)/shard_map/all_to_all | solution.py:295
  103.4 0.2 pack_results.1
  103.6 0.0 copy-start.5
  103.6 0.0 copy-start.9
  103.6 16.3 %all_to_all.35.in_ref = f32[32,8,128]{2,1,0:T(8,128)S(1)} all-to-all(f32[32,8,128]{2,1,0:T(8,128)S(1)} %pack_results.1), channel_id=1, replica_groups=mesh['stream'=32,'cross'=16] {'stream'}, dimensions={0} | all-to-all | bytes 262144 | tf_op jit(solution)/shard_map/all_to_all | solution.py:363
  119.9 1.8 %unpack_cells.1 = (f32[5,2,1024]{2,1,0:T(2,128)}, f32[5,2,1024]{2,1,0:T(2,128)}) custom-call(s32[4,16]{1,0:T(4,128)S(1)} %bitcast.23, s32[4,16]{1,0:T(4,128)S(1)} %bitcast.31, s32[4,16]{1,0:T(4,128)S(1)} %bitcast.27, s32[4,16]{1,0:T(4,128)S(1)} %bitcast.33, f32[2,1024]{1,0:T(2,128)S(1)} %copy-done.3, f32[32,8,128]{2,1,0:T(8,128)S(1)} %all_to_all.35.in_ref), custom_call_target="tpu_custom_call" | custom-call | tf_op jit(solution)/shard_map/unpack_cells/pallas_call | solution.py:364
  (15 shorter events, 0.0 us)
Async XLA Ops:
  0.6 0.7 copy-start.3
  0.6 0.7 copy-start.6
  0.7 0.7 copy-start.4
  0.7 0.7 copy-start.12
  1.3 0.9 copy-start
  2.3 0.9 copy-start.1
  3.2 0.8 copy-start.2
  4.0 0.7 copy-start.8
  4.7 0.7 copy-start.10
  103.6 16.3 %copy-start.5 = (s32[16,4]{0,1:T(4,128)S(1)}, s32[16,4]{0,1:T(4,128)}, u32[]{:S(2)}) copy-start(s32[16,4]{0,1:T(4,128)} %param.13) | copy-start | bytes 772
  103.6 16.3 %copy-start.7 = (s32[16,4]{0,1:T(4,128)S(1)}, s32[16,4]{0,1:T(4,128)}, u32[]{:S(2)}) copy-start(s32[16,4]{0,1:T(4,128)} %param.15) | copy-start | bytes 772
  103.6 16.3 %copy-start.9 = (s32[16,4]{0,1:T(4,128)S(1)}, s32[16,4]{0,1:T(4,128)}, u32[]{:S(2)}) copy-start(s32[16,4]{0,1:T(4,128)} %param.14) | copy-start | bytes 772
  103.6 16.3 %copy-start.11 = (s32[16,4]{0,1:T(4,128)S(1)}, s32[16,4]{0,1:T(4,128)}, u32[]{:S(2)}) copy-start(s32[16,4]{0,1:T(4,128)} %param.16) | copy-start | bytes 772

commit v2 on v1

v2 whole, which is shorter than its diff:
```python
import functools

import jax
import jax.numpy as jnp
from jax import lax
from jax.experimental import pallas as pl
from jax.experimental.pallas import tpu as pltpu
from jax.sharding import PartitionSpec as P

VARS = 5
CELLS = 1024
LINKS = 4
WINDOW = CELLS // LINKS
STREAM = 32
CROSS = 16
PLANES = 2
CHUNKS = 8
GROUPS = 4
LANES = 128
FACE_WEIGHT = 0.25

LOWER = 0
UPPER = 25
SOURCE = 50
ROWS = 110

F32 = jnp.float32
BF16 = jnp.bfloat16
HBM = pl.BlockSpec(memory_space=pltpu.HBM)
SMEM = pl.BlockSpec(memory_space=pltpu.SMEM)
VMEM = pl.BlockSpec(memory_space=pltpu.VMEM)
PARAMS = pltpu.CompilerParams(vmem_limit_bytes=24 * 1024 * 1024)
WIDE = pltpu.CompilerParams(vmem_limit_bytes=62 * 1024 * 1024)
TABLE = pltpu.SMEM((LINKS, CROSS), jnp.int32)
BOTH = ("stream", "cross")


def thirds(x):
    high = x.astype(BF16)
    rest = x - high.astype(F32)
    middle = rest.astype(BF16)
    low = (rest - middle.astype(F32)).astype(BF16)
    return high, middle, low


def copy_in(pairs, sems):
    copies = [pltpu.make_async_copy(src, dst, sems.at[i]) for i, (src, dst) in enumerate(pairs)]
    for copy in copies:
        copy.start()
    return copies


def places(own, link, owner_ref, start_ref, count_ref, flip_ref):
    owner = owner_ref[link, own]
    count = count_ref[link, own]
    turned = jnp.logical_and(flip_ref[link, own] == 1, own > owner)
    bound = jnp.where(turned, count, 0)
    offset = start_ref[link, own] - link * WINDOW
    cell = lax.broadcasted_iota(jnp.int32, (1, WINDOW), 1)
    place = (cell - offset) & (WINDOW - 1)
    return jnp.where(place < bound, count - 1 - place, place)


def onehot(row):
    rows = lax.broadcasted_iota(jnp.int32, (WINDOW, WINDOW), 0)
    return jnp.where(rows == row, 1.0, 0.0).astype(BF16)


def pack_kernel(
    owner_in, start_in, count_in, flip_in, live_in, rhs_in, diagonal_in, lower_in, upper_in,
    out_ref,
    owner_ref, start_ref, count_ref, flip_ref, live_ref, rhs_ref, diagonal_ref, lower_ref, upper_ref,
    rows_ref, sems,
):
    copies = copy_in(
        [
            (lower_in, lower_ref), (upper_in, upper_ref), (rhs_in, rhs_ref),
            (diagonal_in, diagonal_ref), (live_in, live_ref), (owner_in, owner_ref),
            (start_in, start_ref), (count_in, count_ref), (flip_in, flip_ref),
        ],
        sems,
    )
    own = lax.axis_index("cross")
    rows_ref[pl.ds(ROWS, LANES - ROWS), :] = jnp.zeros((LANES - ROWS, CELLS), F32)
    for copy in copies:
        copy.wait()
    cell = lax.broadcasted_iota(jnp.int32, (PLANES, CELLS), 1)
    live = cell < live_ref[own]
    for a in range(VARS):
        for b in range(VARS):
            at = VARS * a + b
            rows_ref[pl.ds(2 * (LOWER + at), 2), :] = lower_ref[a, b]
            rows_ref[pl.ds(2 * (UPPER + at), 2), :] = upper_ref[a, b]
        source = jnp.where(live, rhs_ref[a], 0.0) / diagonal_ref[...]
        rows_ref[pl.ds(2 * (SOURCE + a), 2), :] = source
    for link in range(LINKS):
        place = places(own, link, owner_ref, start_ref, count_ref, flip_ref)
        rest = place & 127
        matrix = onehot(2 * rest + (place >> 7))
        high, middle, low = [
            lax.dot_general(matrix, part, (((1,), (1,)), ((), ())), preferred_element_type=F32)
            for part in thirds(rows_ref[:, link * WINDOW:(link + 1) * WINDOW])
        ]
        out_ref[link * WINDOW:(link + 1) * WINDOW, :] = (low + middle) + high


def entry(system_ref, k, p, at):
    row = 2 * at + p
    return system_ref[k, row:row + 1, :]


def product(system_ref, k, p, at, state):
    out = []
    for a in range(VARS):
        terms = [
            entry(system_ref, k, p, at + VARS * a + b) * state[b] for b in range(VARS)
        ]
        out.append((terms[0] + terms[1]) + (terms[2] + terms[3]) + terms[4])
    return out


def get_rows(ref, k, p):
    return [ref[k, 8 * p + a:8 * p + a + 1, :] for a in range(VARS)]


def put_rows(ref, k, p, rows):
    for a in range(VARS):
        ref[k, 8 * p + a:8 * p + a + 1, :] = rows[a]


def turn(state, by):
    return tuple(pltpu.roll(x, by, 1) for x in state)


def lower_sweep(step):
    state = tuple(jnp.zeros((1, LANES), F32) for _ in range(VARS))
    for group in range(GROUPS):
        if group:
            state = turn(state, 32)
        state = lax.fori_loop(0, CHUNKS, functools.partial(step, group), state, unroll=True)


def upper_sweep(step):
    state = tuple(jnp.zeros((1, LANES), F32) for _ in range(VARS))
    for group in reversed(range(GROUPS)):
        if group < GROUPS - 1:
            state = turn(state, 96)
        state = lax.fori_loop(
            0, CHUNKS, lambda i, x: step(group, CHUNKS - 1 - i, x), state, unroll=True
        )


def merged(ref):
    shape = (CHUNKS * 16, LANES)
    lane = lax.broadcasted_iota(jnp.int32, shape, 1) >> 5
    row = lax.broadcasted_iota(jnp.int32, shape, 0) & 7
    parts = [ref[group].reshape(shape) for group in range(GROUPS)]
    out = jnp.where(lane == 0, parts[0], jnp.where(lane == 1, parts[1], jnp.where(lane == 2, parts[2], parts[3])))
    return jnp.where(row < VARS, out, 0.0)


def upper_pass(system_ref, lowered_ref, coupled_ref, delta_ref):
    def upper(group, k, state):
        for p in reversed(range(PLANES)):
            coupled = product(system_ref, k, p, UPPER, state)
            put_rows(coupled_ref.at[group], k, p, coupled)
            lowered = get_rows(lowered_ref.at[group], k, p)
            state = tuple(w + e for w, e in zip(lowered, coupled))
            put_rows(delta_ref.at[group], k, p, state)
        return state

    upper_sweep(upper)


def face_matrix(owner_ref, count_ref):
    position = lax.axis_index("stream")
    link = position >> 3
    slot = ((position & 7) << 4) + lax.axis_index("cross")
    lane = lax.broadcasted_iota(jnp.int32, (1, LANES), 1)
    source = jnp.full((1, LANES), -1, jnp.int32)
    for block in range(CROSS):
        taken = jnp.where(slot < count_ref[link, block], owner_ref[link, block], -LANES)
        source = jnp.where((lane & 31) == block, (lane & 96) + taken, source)
    rows = lax.broadcasted_iota(jnp.int32, (LANES, LANES), 0)
    return jnp.where(rows == source, FACE_WEIGHT, 0.0).astype(BF16)


def faces_of(field, matrix):
    high, middle, low = [jnp.dot(part, matrix, preferred_element_type=F32) for part in thirds(field)]
    return (low + middle) + high


def solve_kernel(
    owner_in, count_in, in_ref, out_ref,
    owner_ref, count_ref, system_ref, faces_ref, last_ref, solution_ref, residual_ref,
    lowered_ref, coupled_ref, delta_ref, sems,
):
    copies = copy_in([(owner_in, owner_ref), (count_in, count_ref)], sems)
    for k in range(CHUNKS):
        parts = []
        for group in range(GROUPS):
            first = (CHUNKS * group + k) * 32
            parts += [in_ref[pl.ds(first + half, CROSS, stride=2), :] for half in range(2)]
        system_ref[k] = jnp.concatenate(parts, axis=0).T
    for copy in copies:
        copy.wait()
    matrix = face_matrix(owner_ref, count_ref)

    def lower_first(group, k, state):
        for p in range(PLANES):
            along = product(system_ref, k, p, LOWER, state)
            state = tuple(entry(system_ref, k, p, SOURCE + a) + along[a] for a in range(VARS))
            put_rows(lowered_ref.at[group], k, p, state)
        return state

    lower_sweep(lower_first)
    upper_pass(system_ref, lowered_ref, coupled_ref, delta_ref)
    last_ref[...] = merged(coupled_ref).reshape(last_ref.shape)
    first = merged(delta_ref)
    faces_ref[...] = faces_of(first, matrix).reshape(faces_ref.shape)

    def lower_second(group, k, state):
        for p in range(PLANES):
            along = product(system_ref, k, p, LOWER, state)
            lowered = [f + x for f, x in zip(get_rows(faces_ref, k, p), along)]
            put_rows(lowered_ref.at[group], k, p, lowered)
            state = tuple(w + e for w, e in zip(lowered, get_rows(last_ref, k, p)))
        return state

    lower_sweep(lower_second)
    upper_pass(system_ref, lowered_ref, coupled_ref, delta_ref)
    second = merged(delta_ref)
    solution_ref[...] = (first + second).reshape(solution_ref.shape)
    last_ref[...] = merged(coupled_ref).reshape(last_ref.shape)
    lane = lax.broadcasted_iota(jnp.int32, (1, LANES), 1)
    for k in range(CHUNKS):
        if k:
            before = get_rows(last_ref, k - 1, 1)
        else:
            before = [
                jnp.where(lane < 32, 0.0, x) for x in turn(get_rows(last_ref, CHUNKS - 1, 1), 32)
            ]
        put_rows(residual_ref, k, 0, product(system_ref, k, 0, LOWER, before))
        before = get_rows(last_ref, k, 0)
        put_rows(residual_ref, k, 1, product(system_ref, k, 1, LOWER, before))
    residual_ref[...] = residual_ref[...] + faces_of(second, matrix).reshape(residual_ref.shape)

    lane = lax.broadcasted_iota(jnp.int32, (CROSS, LANES), 1) >> 5
    for half in range(2):
        parts = []
        for k in range(4 * half, 4 * half + 4):
            parts += [solution_ref[k], residual_ref[k]]
        turned = jnp.concatenate(parts, axis=0).T
        for group in range(GROUPS):
            face = turned[32 * group:32 * group + 16]
            other = pltpu.roll(turned[32 * group + 16:32 * group + 32], 64, 1)
            for k in range(4):
                first = (CHUNKS * group + 4 * half + k) * CROSS
                out_ref[first:first + CROSS, :] = jnp.where(lane == k, face, other)


def unpack_kernel(
    owner_in, start_in, count_in, flip_in, diagonal_in, in_ref,
    solution_ref, residual_ref,
    owner_ref, start_ref, count_ref, flip_ref, diagonal_ref, rows_ref, sems,
):
    copies = copy_in(
        [
            (owner_in, owner_ref), (start_in, start_ref), (count_in, count_ref),
            (flip_in, flip_ref), (diagonal_in, diagonal_ref),
        ],
        sems,
    )
    own = lax.axis_index("cross")
    group = lax.axis_index("stream") & 3
    face = pl.multiple_of(group * 32, 32)
    other = pl.multiple_of(((group + 2) & 3) * 32, 32)
    for link in range(LINKS):
        rows_ref[link] = in_ref[link * LANES:(link + 1) * LANES, :].T
    for copy in copies:
        copy.wait()
    for link in range(LINKS):
        window = slice(link * WINDOW, (link + 1) * WINDOW)
        matrix = onehot(places(own, link, owner_ref, start_ref, count_ref, flip_ref))
        slots = jnp.concatenate(
            [rows_ref[link, pl.ds(face, 32), :], rows_ref[link, pl.ds(other, 32), :]], axis=1
        )
        high, middle, low = [
            jnp.dot(part, matrix, preferred_element_type=F32) for part in thirds(slots)
        ]
        cells = (low + middle) + high
        for p in range(PLANES):
            residual = cells[16 + 8 * p:16 + 8 * p + VARS] * diagonal_ref[p:p + 1, window]
            for a in range(VARS):
                solution_ref[a, p:p + 1, window] = cells[8 * p + a:8 * p + a + 1]
                residual_ref[a, p:p + 1, window] = residual[a:a + 1]


def shape(*dims):
    return jax.ShapeDtypeStruct(dims, F32)


def local(
    rhs,
    diagonal,
    lower_transfer,
    upper_transfer,
    face_owner,
    face_start,
    face_count,
    face_flip,
    block_cells,
):
    owner, start, count, flip = face_owner.T, face_start.T, face_count.T, face_flip.T
    transfer = pltpu.VMEM((VARS, VARS, PLANES, CELLS), F32)
    planes = pltpu.VMEM((PLANES, CELLS), F32)
    packed = pl.pallas_call(
        pack_kernel,
        out_shape=shape(CELLS, LANES),
        in_specs=[HBM] * 9,
        out_specs=VMEM,
        scratch_shapes=[TABLE] * 4
        + [
            pltpu.SMEM((CROSS,), jnp.int32), pltpu.VMEM((VARS, PLANES, CELLS), F32), planes,
            transfer, transfer, pltpu.VMEM((LANES, CELLS), F32), pltpu.SemaphoreType.DMA((9,)),
        ],
        compiler_params=WIDE,
        name="pack_cells",
    )(
        owner, start, count, flip,
        block_cells,
        rhs.transpose(1, 0, 2),
        diagonal,
        lower_transfer.transpose(1, 2, 0, 3),
        upper_transfer.transpose(1, 2, 0, 3),
    )
    arrived = lax.all_to_all(packed.reshape(STREAM * CROSS, 2, LANES), BOTH, 0, 0, tiled=True)

    passes = pltpu.VMEM((GROUPS, CHUNKS, 16, LANES), F32)
    chunks = pltpu.VMEM((CHUNKS, 16, LANES), F32)
    results = pl.pallas_call(
        solve_kernel,
        out_shape=shape(STREAM * CROSS, LANES),
        in_specs=[HBM, HBM, VMEM],
        out_specs=VMEM,
        scratch_shapes=[TABLE] * 2
        + [pltpu.VMEM((CHUNKS, LANES, LANES), F32)]
        + [chunks] * 4
        + [passes] * 3
        + [pltpu.SemaphoreType.DMA((2,))],
        compiler_params=PARAMS,
        name="solve_cells",
    )(owner, count, arrived.reshape(CELLS, LANES))
    returned = lax.all_to_all(results.reshape(STREAM * CROSS, 1, LANES), BOTH, 0, 0, tiled=True)
    outs = pl.pallas_call(
        unpack_kernel,
        out_shape=[shape(VARS, PLANES, CELLS)] * 2,
        in_specs=[HBM] * 5 + [VMEM],
        out_specs=[VMEM] * 2,
        scratch_shapes=[TABLE] * 4
        + [planes, pltpu.VMEM((LINKS, LANES, LANES), F32), pltpu.SemaphoreType.DMA((5,))],
        compiler_params=PARAMS,
        name="unpack_cells",
    )(owner, start, count, flip, diagonal, returned.reshape(STREAM * CROSS, LANES))
    return tuple(x.transpose(1, 0, 2) for x in outs)


def solution(mesh):
    return jax.shard_map(
        local,
        mesh=mesh,
        in_specs=(
            P("stream", None, "cross"),
            P("stream", "cross"),
            P("stream", None, None, "cross"),
            P("stream", None, None, "cross"),
            P(),
            P(),
            P(),
            P(),
            P(),
        ),
        out_specs=(P("stream", None, "cross"), P("stream", None, "cross")),
        check_vma=False,
    )
```

time: 122 us -> 103 us (0.84)
  blocking collectives: 107 us -> 94.2 us
  local copies, waits for them, and re-layouts: 4.71 us -> 0.03 us
    all_to_all x6 -> x2, blocking collectives: 107 us -> 94.2 us  [the longest x1 59.8 us: local(): lax.all_to_all(packed.reshape(STREAM * CROSS, 2, LANES), BOTH, 0, 0, tile...]
    unnamed x26 -> x10, local copies, waits for them, and re-layouts: 4.71 us -> 0.03 us
    pallas_call x6 -> x2, Pallas kernels: 7.6 us -> 6.6 us  [the longest x1 3.96 us: local(): pl.pallas_call(solve_kernel, out_shape=shape(STREAM * CROSS, LANES), in_s...]
where the time goes in v2:
time: 103 us
  blocking collectives  94.2 us (91%)
  Pallas kernels  8.33 us (8%)
    all_to_all x1, blocking collectives, local(): lax.all_to_all(packed.reshape(STREAM * CROSS, 2, LANES), BOTH, 0, 0, tile...  59.8 us
    all_to_all x1, blocking collectives, local(): lax.all_to_all(results.reshape(STREAM * CROSS, 1, LANES), BOTH, 0, 0, til...  34.4 us
    pallas_call x1, Pallas kernels, local(): pl.pallas_call(solve_kernel, out_shape=shape(STREAM * CROSS, LANES), in_s...  3.96 us
    pallas_call x1, Pallas kernels, local(): pl.pallas_call(pack_kernel, out_shape=shape(CELLS, LANES), in_specs=[HBM]...  2.64 us

profile of v2, /device:TPU:1, one launch (start us, length us, event | category | flops | bytes accessed | tf_op | source)
XLA Modules:
  0.0 103.2 jit_solution(18325216039544789662)
XLA Ops:
  0.6 2.6 %pack_cells.1 = f32[1024,128]{1,0:T(8,128)} custom-call(s32[4,16]{1,0:T(4,128)} %bitcast.18, s32[4,16]{1,0:T(4,128)} %bitcast.24, s32[4,16]{1,0:T(4,128)} %bitcast.21, s32[4,16]{1,0:T(4,128)} %bitcast.26, s32[16]{0:T(128)} %live_in.1, f32[5,2,1024]{2,1,0:T(2,128)} %bitcast.31, f32[2,1024]{1,0:T(2,128)} %diagonal_in.3, f32[5,5,2,1024]{3,2,1,0:T(2,128)} %bitcast.29, ...), custom_call_target="tpu_custom_call" | custom-call | tf_op jit(solution)/shard_map/pack_cells/pallas_call | solution.py:317
  3.3 0.0 copy-start.1
  3.3 0.0 copy-start.2
  3.3 59.8 %all_to_all.10 = f32[512,2,128]{2,1,0:T(2,128)S(1)} all-to-all(f32[512,2,128]{2,1,0:T(2,128)} %bitcast.28), channel_id=1, replica_groups=mesh['stream'=32,'cross'=16] {'stream','cross'}, dimensions={0} | all-to-all | bytes 1048576 | tf_op jit(solution)/shard_map/all_to_all | solution.py:337
  63.1 0.0 copy-done.1
  63.1 0.0 copy-done.2
  63.1 4.0 %solve_cells.1 = f32[512,128]{1,0:T(8,128)S(1)} custom-call(s32[4,16]{1,0:T(4,128)S(1)} %bitcast.19, s32[4,16]{1,0:T(4,128)S(1)} %bitcast.22, f32[1024,128]{1,0:T(8,128)S(1)} %bitcast.15), custom_call_target="tpu_custom_call" | custom-call | tf_op jit(solution)/shard_map/solve_cells/pallas_call | solution.py:341
  67.1 0.0 copy-start
  67.1 0.0 copy-start.3
  67.1 0.0 copy-start.4
  67.1 34.4 %all_to_all.11 = f32[512,1,128]{2,1,0:T(1,128)S(1)} all-to-all(f32[512,1,128]{2,1,0:T(1,128)S(1)} %bitcast.16), channel_id=1, replica_groups=mesh['stream'=32,'cross'=16] {'stream','cross'}, dimensions={0} | all-to-all | bytes 524288 | tf_op jit(solution)/shard_map/all_to_all | solution.py:354
  101.5 0.0 copy-done
  101.5 0.0 copy-done.3
  101.5 0.0 copy-done.4
  101.5 1.7 %unpack_cells.1 = (f32[5,2,1024]{2,1,0:T(2,128)}, f32[5,2,1024]{2,1,0:T(2,128)}) custom-call(s32[4,16]{1,0:T(4,128)S(1)} %bitcast.20, s32[4,16]{1,0:T(4,128)S(1)} %bitcast.25, s32[4,16]{1,0:T(4,128)S(1)} %bitcast.23, s32[4,16]{1,0:T(4,128)S(1)} %bitcast.27, f32[2,1024]{1,0:T(2,128)S(1)} %copy-done, f32[512,128]{1,0:T(8,128)S(1)} %bitcast.17), custom_call_target="tpu_custom_call" | custom-call | tf_op jit(solution)/shard_map/unpack_cells/pallas_call | solution.py:355
Async XLA Ops:
  3.3 59.9 %copy-start.1 = (s32[16,4]{0,1:T(4,128)S(1)}, s32[16,4]{0,1:T(4,128)}, u32[]{:S(2)}) copy-start(s32[16,4]{0,1:T(4,128)} %param.13) | copy-start | bytes 772
  3.3 59.8 %copy-start.2 = (s32[16,4]{0,1:T(4,128)S(1)}, s32[16,4]{0,1:T(4,128)}, u32[]{:S(2)}) copy-start(s32[16,4]{0,1:T(4,128)} %param.15) | copy-start | bytes 772
  67.1 34.4 %copy-start = (f32[2,1024]{1,0:T(2,128)S(1)}, f32[2,1024]{1,0:T(2,128)}, u32[]{:S(2)}) copy-start(f32[2,1024]{1,0:T(2,128)} %diagonal_in.3) | copy-start | bytes 24580
  67.1 34.4 %copy-start.3 = (s32[16,4]{0,1:T(4,128)S(1)}, s32[16,4]{0,1:T(4,128)}, u32[]{:S(2)}) copy-start(s32[16,4]{0,1:T(4,128)} %param.14) | copy-start | bytes 772
  67.1 34.4 %copy-start.4 = (s32[16,4]{0,1:T(4,128)S(1)}, s32[16,4]{0,1:T(4,128)}, u32[]{:S(2)}) copy-start(s32[16,4]{0,1:T(4,128)} %param.16) | copy-start | bytes 772

commit v3 on v2

v3 whole, which is shorter than its diff:
```python
import functools

import jax
import jax.numpy as jnp
from jax import lax
from jax.experimental import pallas as pl
from jax.experimental.pallas import tpu as pltpu
from jax.sharding import PartitionSpec as P

VARS = 5
CELLS = 1024
LINKS = 4
WINDOW = CELLS // LINKS
STREAM = 32
CROSS = 16
PLANES = 2
CHUNKS = 8
GROUPS = 4
LANES = 128
FACE_WEIGHT = 0.25

LOWER = 0
UPPER = 25
SOURCE = 50
ROWS = 110
KEPT = 28
PIECES = 7

F32 = jnp.float32
BF16 = jnp.bfloat16
HBM = pl.BlockSpec(memory_space=pltpu.HBM)
SMEM = pl.BlockSpec(memory_space=pltpu.SMEM)
VMEM = pl.BlockSpec(memory_space=pltpu.VMEM)
PARAMS = pltpu.CompilerParams(vmem_limit_bytes=24 * 1024 * 1024)
WIDE = pltpu.CompilerParams(vmem_limit_bytes=62 * 1024 * 1024)
TABLE = pltpu.SMEM((LINKS, CROSS), jnp.int32)


def thirds(x):
    high = x.astype(BF16)
    rest = x - high.astype(F32)
    middle = rest.astype(BF16)
    low = (rest - middle.astype(F32)).astype(BF16)
    return jnp.concatenate([high, middle, low], axis=0)


def times(x, matrix):
    n = x.shape[0]
    parts = jnp.dot(thirds(x), matrix, preferred_element_type=F32)
    return (parts[2 * n:] + parts[n:2 * n]) + parts[:n]


def copy_in(pairs, sems):
    copies = [pltpu.make_async_copy(src, dst, sems.at[i]) for i, (src, dst) in enumerate(pairs)]
    for copy in copies:
        copy.start()
    return copies


def slots_of(own, link, owner_ref, start_ref, count_ref, flip_ref):
    owner = owner_ref[link, own]
    count = count_ref[link, own]
    turned = jnp.logical_and(flip_ref[link, own] == 1, own > owner)
    bound = jnp.where(turned, count, 0)
    offset = start_ref[link, own] - link * WINDOW
    cell = lax.broadcasted_iota(jnp.int32, (1, WINDOW), 1)
    place = (cell - offset) & (WINDOW - 1)
    place = jnp.where(place < bound, count - 1 - place, place)
    rest = place & 127
    return ((rest >> 4) << 5) + ((place >> 7) << 4) + (rest & 15)


def onehot(row):
    rows = lax.broadcasted_iota(jnp.int32, (WINDOW, WINDOW), 0)
    return jnp.where(rows == row, 1.0, 0.0).astype(BF16)


def pack_kernel(
    owner_in, start_in, count_in, flip_in, live_in, rhs_in, diagonal_in, lower_in, upper_in,
    out_ref, slots_ref,
    owner_ref, start_ref, count_ref, flip_ref, live_ref, rhs_ref, diagonal_ref, lower_ref, upper_ref,
    rows_ref, matrix_ref, sems,
):
    copies = copy_in(
        [
            (owner_in, owner_ref), (start_in, start_ref), (count_in, count_ref),
            (flip_in, flip_ref), (live_in, live_ref), (rhs_in, rhs_ref),
            (diagonal_in, diagonal_ref), (lower_in, lower_ref), (upper_in, upper_ref),
        ],
        sems,
    )
    own = lax.axis_index("cross")
    rows_ref[pl.ds(ROWS, LANES - ROWS), :] = jnp.zeros((LANES - ROWS, CELLS), F32)
    for copy in copies[:5]:
        copy.wait()
    for link in range(LINKS):
        slots = slots_of(own, link, owner_ref, start_ref, count_ref, flip_ref)
        slots_ref[link:link + 1, :] = slots
        matrix_ref[link] = onehot(slots)
    for copy in copies[5:]:
        copy.wait()
    cell = lax.broadcasted_iota(jnp.int32, (PLANES, CELLS), 1)
    live = cell < live_ref[own]
    for a in range(VARS):
        for b in range(VARS):
            at = VARS * a + b
            rows_ref[pl.ds(2 * (LOWER + at), 2), :] = lower_ref[a, b]
            rows_ref[pl.ds(2 * (UPPER + at), 2), :] = upper_ref[a, b]
        source = jnp.where(live, rhs_ref[a], 0.0) / diagonal_ref[...]
        rows_ref[pl.ds(2 * (SOURCE + a), 2), :] = source
    for link in range(LINKS):
        parts = lax.dot_general(
            matrix_ref[link],
            thirds(rows_ref[:, link * WINDOW:(link + 1) * WINDOW]),
            (((1,), (1,)), ((), ())),
            preferred_element_type=F32,
        )
        out_ref[link * WINDOW:(link + 1) * WINDOW, :] = (
            parts[:, 2 * LANES:] + parts[:, LANES:2 * LANES]
        ) + parts[:, :LANES]


def entry(system_ref, k, p, at):
    row = 2 * at + p
    return system_ref[k, row:row + 1, :]


def terms(system_ref, k, p, at, state):
    return [
        [entry(system_ref, k, p, at + VARS * a + b) * state[b] for b in range(VARS)]
        for a in range(VARS)
    ]


def total(rows, first=None):
    if first is None:
        return tuple((t[0] + t[1]) + (t[2] + t[3]) + t[4] for t in rows)
    return tuple(((x + t[0]) + (t[1] + t[2])) + (t[3] + t[4]) for x, t in zip(first, rows))


def get_rows(ref, k, p):
    return [ref[k, 8 * p + a:8 * p + a + 1, :] for a in range(VARS)]


def put_rows(ref, k, p, rows):
    for a in range(VARS):
        ref[k, 8 * p + a:8 * p + a + 1, :] = rows[a]


def turn(state, by):
    return tuple(pltpu.roll(x, by, 1) for x in state)


def lower_sweep(step):
    state = tuple(jnp.zeros((1, LANES), F32) for _ in range(VARS))
    for group in range(GROUPS):
        if group:
            state = turn(state, 32)
        state = lax.fori_loop(0, CHUNKS, functools.partial(step, group), state, unroll=True)


def upper_sweep(step):
    state = tuple(jnp.zeros((1, LANES), F32) for _ in range(VARS))
    for group in reversed(range(GROUPS)):
        if group < GROUPS - 1:
            state = turn(state, 96)
        state = lax.fori_loop(
            0, CHUNKS, lambda i, x: step(group, CHUNKS - 1 - i, x), state, unroll=True
        )


def merged(ref):
    shape = (CHUNKS * 16, LANES)
    lane = lax.broadcasted_iota(jnp.int32, shape, 1) >> 5
    row = lax.broadcasted_iota(jnp.int32, shape, 0) & 7
    parts = [ref[group].reshape(shape) for group in range(GROUPS)]
    out = jnp.where(lane == 0, parts[0], jnp.where(lane == 1, parts[1], jnp.where(lane == 2, parts[2], parts[3])))
    return jnp.where(row < VARS, out, 0.0)


def upper_pass(system_ref, lowered_ref, coupled_ref, delta_ref):
    def upper(group, k, state):
        for p in reversed(range(PLANES)):
            coupled = terms(system_ref, k, p, UPPER, state)
            put_rows(coupled_ref.at[group], k, p, total(coupled))
            state = total(coupled, get_rows(lowered_ref.at[group], k, p))
            put_rows(delta_ref.at[group], k, p, state)
        return state

    upper_sweep(upper)


def face_matrix(owner_ref, count_ref):
    position = lax.axis_index("stream")
    link = position >> 3
    slot = ((position & 7) << 4) + lax.axis_index("cross")
    lane = lax.broadcasted_iota(jnp.int32, (1, LANES), 1)
    source = jnp.full((1, LANES), -1, jnp.int32)
    for block in range(CROSS):
        taken = jnp.where(slot < count_ref[link, block], owner_ref[link, block], -LANES)
        source = jnp.where((lane & 31) == block, (lane & 96) + taken, source)
    rows = lax.broadcasted_iota(jnp.int32, (LANES, LANES), 0)
    return jnp.where(rows == source, FACE_WEIGHT, 0.0).astype(BF16)


def faces_kernel(in_ref, out_ref):
    lane = lax.broadcasted_iota(jnp.int32, (CROSS, LANES), 1)
    for row in range(KEPT):
        piece = row % PIECES
        first = 32 * (KEPT + row // PIECES)
        spare = pltpu.roll(in_ref[first:first + CROSS, :], ROWS - 16 * piece, 1)
        own = in_ref[32 * row:32 * row + CROSS, :]
        out_ref[pl.ds(row, CROSS, stride=KEPT), :] = jnp.where(lane < ROWS, own, spare)


def face_rows(face_ref, chunk):
    if chunk < KEPT:
        return face_ref[pl.ds(chunk, CROSS, stride=KEPT), :]
    piece_of = lax.broadcasted_iota(jnp.int32, (CROSS, LANES), 1) >> 4
    out = jnp.zeros((CROSS, LANES), F32)
    for piece in range(PIECES):
        row = PIECES * (chunk - KEPT) + piece
        moved = pltpu.roll(
            face_ref[pl.ds(row, CROSS, stride=KEPT), :], LANES - ROWS + 16 * piece, 1
        )
        out = jnp.where(piece_of == piece, moved, out)
    return out


def solve_kernel(
    owner_in, count_in, in_ref, face_ref, out_ref, send_ref,
    owner_ref, count_ref, system_ref, faces_ref, last_ref, solution_ref, residual_ref,
    lowered_ref, coupled_ref, delta_ref, values_ref, sems,
):
    values_ref[160:, :] = jnp.zeros((96, LANES), F32)
    copies = copy_in([(owner_in, owner_ref), (count_in, count_ref)], sems)
    for k in range(CHUNKS):
        parts = []
        for group in range(GROUPS):
            chunk = CHUNKS * group + k
            parts += [
                face_rows(face_ref, chunk),
                in_ref[32 * chunk + 16:32 * chunk + 32, :],
            ]
        system_ref[k] = jnp.concatenate(parts, axis=0).T
    for copy in copies:
        copy.wait()
    matrix = face_matrix(owner_ref, count_ref)

    def lower_first(group, k, state):
        for p in range(PLANES):
            along = terms(system_ref, k, p, LOWER, state)
            state = total(along, [entry(system_ref, k, p, SOURCE + a) for a in range(VARS)])
            put_rows(lowered_ref.at[group], k, p, state)
        return state

    lower_sweep(lower_first)
    upper_pass(system_ref, lowered_ref, coupled_ref, delta_ref)
    last_ref[...] = merged(coupled_ref).reshape(last_ref.shape)
    first = merged(delta_ref)
    faces_ref[...] = times(first, matrix).reshape(faces_ref.shape)

    def lower_second(group, k, state):
        for p in range(PLANES):
            along = terms(system_ref, k, p, LOWER, state)
            faces = get_rows(faces_ref, k, p)
            put_rows(lowered_ref.at[group], k, p, total(along, faces))
            state = total(along, [f + e for f, e in zip(faces, get_rows(last_ref, k, p))])
        return state

    lower_sweep(lower_second)
    upper_pass(system_ref, lowered_ref, coupled_ref, delta_ref)
    second = merged(delta_ref)
    solution_ref[...] = (first + second).reshape(solution_ref.shape)
    last_ref[...] = merged(coupled_ref).reshape(last_ref.shape)
    lane = lax.broadcasted_iota(jnp.int32, (1, LANES), 1)
    for k in range(CHUNKS):
        if k:
            before = get_rows(last_ref, k - 1, 1)
        else:
            before = [
                jnp.where(lane < 32, 0.0, x) for x in turn(get_rows(last_ref, CHUNKS - 1, 1), 32)
            ]
        put_rows(residual_ref, k, 0, total(terms(system_ref, k, 0, LOWER, before)))
        before = get_rows(last_ref, k, 0)
        put_rows(residual_ref, k, 1, total(terms(system_ref, k, 1, LOWER, before)))
    residual_ref[...] = residual_ref[...] + times(second, matrix).reshape(residual_ref.shape)

    for k in range(CHUNKS):
        out_ref[k, 0:16, :] = solution_ref[k]
        out_ref[k, 16:32, :] = residual_ref[k]
    for k in range(CHUNKS):
        for g in range(4):
            at = 5 * (4 * k + g)
            values_ref[at:at + VARS, :] = out_ref[k, 8 * g:8 * g + VARS, :]
    turned = values_ref[0:LANES, :].T
    others = values_ref[LANES:2 * LANES, :].T
    lane_group = lax.broadcasted_iota(jnp.int32, (CROSS, LANES), 1) >> 5
    fifth = others[0:CROSS]
    for group in range(GROUPS):
        rows = slice(32 * group, 32 * group + CROSS)
        send_ref[pl.ds(group, CROSS, stride=5), :] = turned[rows]
        if group:
            fifth = jnp.where(lane_group == group, pltpu.roll(others[rows], 32 * group, 1), fifth)
    send_ref[pl.ds(4, CROSS, stride=5), :] = fifth


def regroup(parts):
    lane = lax.broadcasted_iota(jnp.int32, parts[0].shape, 1)
    first_half = lane < 64
    even = (lane & 32) == 0
    half = [None] * 4
    for i in range(2):
        x, y = parts[i], parts[i + 2]
        half[i] = jnp.where(first_half, x, pltpu.roll(y, 64, 1))
        half[i + 2] = jnp.where(first_half, pltpu.roll(x, 64, 1), y)
    out = [None] * 4
    for i in (0, 2):
        x, y = half[i], half[i + 1]
        out[i] = jnp.where(even, x, pltpu.roll(y, 32, 1))
        out[i + 1] = jnp.where(even, pltpu.roll(x, 96, 1), y)
    return out


def join_kernel(in_ref, face_ref, out_ref, values_ref):
    lane = lax.broadcasted_iota(jnp.int32, (8, LANES), 1)
    returned = (lane & 16) == 0
    blank = jnp.zeros((16, LANES), F32)
    fifth = face_ref[pl.ds(4, CROSS, stride=5), :]
    parts = []
    others = []
    for group in range(GROUPS):
        parts += [face_ref[pl.ds(group, CROSS, stride=5), :], blank]
        others += [pltpu.roll(fifth, (LANES - 32 * group) % LANES, 1) if group else fifth, blank]
    values_ref[0:LANES, :] = jnp.concatenate(parts, axis=0).T
    values_ref[LANES:2 * LANES, :] = jnp.concatenate(others, axis=0).T
    for k in range(CHUNKS):
        tiles = []
        for g in range(4):
            at = 5 * (4 * k + g)
            tiles.append(jnp.where(returned, values_ref[at:at + 8, :], in_ref[k, 8 * g:8 * g + 8, :]))
        for group, tile in enumerate(regroup(tiles)):
            out_ref[CHUNKS * group + k] = tile


def unpack_kernel(slots_ref, diagonal_ref, in_ref, solution_ref, residual_ref, rows_ref):
    for column in range(8):
        tiles = regroup([in_ref[4 * column + e] for e in range(4)])
        for g, tile in enumerate(tiles):
            rows_ref[8 * g:8 * g + 8, LANES * column:LANES * (column + 1)] = tile
    for link in range(LINKS):
        window = slice(link * WINDOW, (link + 1) * WINDOW)
        cells = times(rows_ref[:, window], onehot(slots_ref[link:link + 1, :]))
        for p in range(PLANES):
            residual = cells[16 + 8 * p:16 + 8 * p + VARS] * diagonal_ref[p:p + 1, window]
            for a in range(VARS):
                solution_ref[a, p:p + 1, window] = cells[8 * p + a:8 * p + a + 1]
                residual_ref[a, p:p + 1, window] = residual[a:a + 1]


def shape(*dims):
    return jax.ShapeDtypeStruct(dims, F32)


def local(
    rhs,
    diagonal,
    lower_transfer,
    upper_transfer,
    face_owner,
    face_start,
    face_count,
    face_flip,
    block_cells,
):
    owner, start, count, flip = face_owner.T, face_start.T, face_count.T, face_flip.T
    transfer = pltpu.VMEM((VARS, VARS, PLANES, CELLS), F32)
    planes = pltpu.VMEM((PLANES, CELLS), F32)
    packed, slots = pl.pallas_call(
        pack_kernel,
        out_shape=[shape(CELLS, LANES), jax.ShapeDtypeStruct((LINKS, WINDOW), jnp.int32)],
        in_specs=[HBM] * 9,
        out_specs=[VMEM] * 2,
        scratch_shapes=[TABLE] * 4
        + [
            pltpu.SMEM((CROSS,), jnp.int32), pltpu.VMEM((VARS, PLANES, CELLS), F32), planes,
            transfer, transfer, pltpu.VMEM((LANES, CELLS), F32),
            pltpu.VMEM((LINKS, WINDOW, WINDOW), BF16), pltpu.SemaphoreType.DMA((9,)),
        ],
        compiler_params=WIDE,
        name="pack_cells",
    )(
        owner, start, count, flip,
        block_cells,
        rhs.transpose(1, 0, 2),
        diagonal,
        lower_transfer.transpose(1, 2, 0, 3),
        upper_transfer.transpose(1, 2, 0, 3),
    )
    arrived = lax.all_to_all(packed.reshape(STREAM, 32, LANES), "stream", 0, 0, tiled=True)
    arrived = arrived.reshape(CELLS, LANES)
    faces = pl.pallas_call(
        faces_kernel,
        out_shape=shape(CROSS * KEPT, LANES),
        in_specs=[VMEM],
        out_specs=VMEM,
        compiler_params=PARAMS,
        name="take_faces",
    )(arrived)
    faces = lax.all_to_all(faces.reshape(CROSS * KEPT // 4, 4, LANES), "cross", 0, 0, tiled=True)

    passes = pltpu.VMEM((GROUPS, CHUNKS, 16, LANES), F32)
    chunks = pltpu.VMEM((CHUNKS, 16, LANES), F32)
    results, faces = pl.pallas_call(
        solve_kernel,
        out_shape=[shape(CHUNKS, 32, LANES), shape(5 * CROSS, LANES)],
        in_specs=[HBM, HBM, VMEM, VMEM],
        out_specs=[VMEM, VMEM],
        scratch_shapes=[TABLE] * 2
        + [pltpu.VMEM((CHUNKS, LANES, LANES), F32)]
        + [chunks] * 4
        + [passes] * 3
        + [pltpu.VMEM((2 * LANES, LANES), F32), pltpu.SemaphoreType.DMA((2,))],
        compiler_params=PARAMS,
        name="solve_cells",
    )(owner, count, arrived, faces.reshape(CROSS * KEPT, LANES))
    faces = lax.all_to_all(faces.reshape(5 * CROSS, 1, LANES), "cross", 0, 0, tiled=True)
    results = pl.pallas_call(
        join_kernel,
        out_shape=shape(STREAM, 8, LANES),
        in_specs=[VMEM, VMEM],
        out_specs=VMEM,
        scratch_shapes=[pltpu.VMEM((2 * LANES, LANES), F32)],
        compiler_params=PARAMS,
        name="join_faces",
    )(results, faces.reshape(5 * CROSS, LANES))
    returned = lax.all_to_all(results, "stream", 0, 0, tiled=True)
    outs = pl.pallas_call(
        unpack_kernel,
        out_shape=[shape(VARS, PLANES, CELLS)] * 2,
        in_specs=[VMEM] * 3,
        out_specs=[VMEM] * 2,
        scratch_shapes=[pltpu.VMEM((32, CELLS), F32)],
        compiler_params=PARAMS,
        name="unpack_cells",
    )(slots, diagonal, returned)
    return tuple(x.transpose(1, 0, 2) for x in outs)


def solution(mesh):
    return jax.shard_map(
        local,
        mesh=mesh,
        in_specs=(
            P("stream", None, "cross"),
            P("stream", "cross"),
            P("stream", None, None, "cross"),
            P("stream", None, None, "cross"),
            P(),
            P(),
            P(),
            P(),
            P(),
        ),
        out_specs=(P("stream", None, "cross"), P("stream", None, "cross")),
        check_vma=False,
    )
```

time: 103 us -> 91.6 us (0.89)
  blocking collectives: 94.2 us -> 82 us
    all_to_all x2 -> x4, blocking collectives: 94.2 us -> 82 us  [the longest x1 26.7 us: local(): lax.all_to_all(faces.reshape(CROSS * KEPT // 4, 4, LANES), 'cross', 0, 0,...]
    pallas_call x2 -> x4, Pallas kernels: 6.6 us -> 7.47 us  [the longest x1 4.51 us: local(): pl.pallas_call(solve_kernel, out_shape=[shape(CHUNKS, 32, LANES), shape(5...]
where the time goes in v3:
time: 91.6 us; the launch traced here: 91.2 us
  blocking collectives  82 us (90%)
  Pallas kernels  8.49 us (9%)
    all_to_all x1, blocking collectives, local(): lax.all_to_all(faces.reshape(CROSS * KEPT // 4, 4, LANES), 'cross', 0, 0,...  26.7 us
    all_to_all x1, blocking collectives, local(): lax.all_to_all(packed.reshape(STREAM, 32, LANES), 'stream', 0, 0, tiled=T...  22.2 us
    all_to_all x1, blocking collectives, local(): lax.all_to_all(faces.reshape(5 * CROSS, 1, LANES), 'cross', 0, 0, tiled=T...  20.3 us
    all_to_all x1, blocking collectives, local(): returned = lax.all_to_all(results, 'stream', 0, 0, tiled=True)  12.8 us
    pallas_call x1, Pallas kernels, local(): pl.pallas_call(solve_kernel, out_shape=[shape(CHUNKS, 32, LANES), shape(5...  4.51 us
    pallas_call x1, Pallas kernels, local(): pl.pallas_call(pack_kernel, out_shape=[shape(CELLS, LANES), jax.ShapeDtyp...  2.49 us

profile of v3, /device:TPU:1, one launch (start us, length us, event | category | flops | bytes accessed | tf_op | source)
XLA Modules:
  0.0 91.2 jit_solution(14008010205730936083)
XLA Ops:
  0.6 2.5 %pack_cells.1 = (f32[1024,128]{1,0:T(8,128)}, s32[4,256]{1,0:T(4,128)}) custom-call(s32[4,16]{1,0:T(4,128)} %bitcast.23, s32[4,16]{1,0:T(4,128)} %bitcast.31, s32[4,16]{1,0:T(4,128)} %bitcast.25, s32[4,16]{1,0:T(4,128)} %bitcast.32, s32[16]{0:T(128)} %live_in.1, f32[5,2,1024]{2,1,0:T(2,128)} %bitcast.30, f32[2,1024]{1,0:T(2,128)} %diagonal_ref.1, ...), custom_call_target="tpu_custom_call" | custom-call | tf_op jit(solution)/shard_map/pack_cells/pallas_call | solution.py:379
  3.1 22.2 %all_to_all.20 = f32[32,32,128]{2,1,0:T(8,128)S(1)} all-to-all(f32[32,32,128]{2,1,0:T(8,128)} %bitcast.27), channel_id=1, replica_groups=mesh['stream'=32,'cross'=16] {'stream'}, dimensions={0} | all-to-all | bytes 1048576 | tf_op jit(solution)/shard_map/all_to_all | solution.py:400
  25.3 0.1 take_faces.1
  25.4 0.0 copy-start.1
  25.4 0.0 copy-start.2
  25.4 26.7 %all_to_all.21 = f32[112,4,128]{2,1,0:T(4,128)S(1)} all-to-all(f32[112,4,128]{2,1,0:T(4,128)S(1)} %bitcast.20), channel_id=1, replica_groups=mesh['stream'=32,'cross'=16] {'cross'}, dimensions={0} | all-to-all | bytes 458752 | tf_op jit(solution)/shard_map/all_to_all | solution.py:410
  52.2 0.0 copy-done.1
  52.2 0.0 copy-done.2
  52.2 4.5 %solve_cells.1 = (f32[8,32,128]{2,1,0:T(8,128)S(1)}, f32[80,128]{1,0:T(8,128)S(1)}) custom-call(s32[4,16]{1,0:T(4,128)S(1)} %bitcast.24, s32[4,16]{1,0:T(4,128)S(1)} %bitcast.26, f32[1024,128]{1,0:T(8,128)S(1)} %bitcast.18, f32[448,128]{1,0:T(8,128)S(1)} %bitcast.19), custom_call_target="tpu_custom_call" | custom-call | tf_op jit(solution)/shard_map/solve_cells/pallas_call | solution.py:414
  56.7 20.3 %all_to_all.22 = f32[80,1,128]{2,1,0:T(1,128)S(1)} all-to-all(f32[80,1,128]{2,1,0:T(1,128)S(1)} %bitcast.22), channel_id=1, replica_groups=mesh['stream'=32,'cross'=16] {'cross'}, dimensions={0} | all-to-all | bytes 81920 | tf_op jit(solution)/shard_map/all_to_all | solution.py:427
  77.0 0.4 join_faces.1
  77.4 0.0 copy-start
  77.4 0.0 copy-start.3
  77.4 12.8 %all_to_all.23.in_ref = f32[32,8,128]{2,1,0:T(8,128)S(1)} all-to-all(f32[32,8,128]{2,1,0:T(8,128)S(1)} %join_faces.1), channel_id=1, replica_groups=mesh['stream'=32,'cross'=16] {'stream'}, dimensions={0} | all-to-all | bytes 262144 | tf_op jit(solution)/shard_map/all_to_all | solution.py:437
  90.2 0.0 copy-done
  90.2 0.0 copy-done.3
  90.2 1.0 %unpack_cells.1 = (f32[5,2,1024]{2,1,0:T(2,128)}, f32[5,2,1024]{2,1,0:T(2,128)}) custom-call(s32[4,256]{1,0:T(4,128)S(1)} %copy-done.3, f32[2,1024]{1,0:T(2,128)S(1)} %copy-done, f32[32,8,128]{2,1,0:T(8,128)S(1)} %all_to_all.23.in_ref), custom_call_target="tpu_custom_call" | custom-call | tf_op jit(solution)/shard_map/unpack_cells/pallas_call | solution.py:438
Async XLA Ops:
  25.4 26.8 %copy-start.1 = (s32[16,4]{0,1:T(4,128)S(1)}, s32[16,4]{0,1:T(4,128)}, u32[]{:S(2)}) copy-start(s32[16,4]{0,1:T(4,128)} %param.13) | copy-start | bytes 772
  25.4 26.7 %copy-start.2 = (s32[16,4]{0,1:T(4,128)S(1)}, s32[16,4]{0,1:T(4,128)}, u32[]{:S(2)}) copy-start(s32[16,4]{0,1:T(4,128)} %param.15) | copy-start | bytes 772
  77.4 12.8 %copy-start = (f32[2,1024]{1,0:T(2,128)S(1)}, f32[2,1024]{1,0:T(2,128)}, u32[]{:S(2)}) copy-start(f32[2,1024]{1,0:T(2,128)} %diagonal_ref.1) | copy-start | bytes 24580
  77.4 12.8 %copy-start.3 = (s32[4,256]{1,0:T(4,128)S(1)}, s32[4,256]{1,0:T(4,128)}, u32[]{:S(2)}) copy-start(s32[4,256]{1,0:T(4,128)} %get-tuple-element.8.slots_ref) | copy-start | bytes 12292

commit v4 on v3

--- a/solution.py
+++ b/solution.py
@@ -120,74 +120,63 @@
         ) + parts[:, :LANES]
 
 
-def entry(system_ref, k, p, at):
-    row = 2 * at + p
-    return system_ref[k, row:row + 1, :]
-
-
-def terms(system_ref, k, p, at, state):
-    return [
-        [entry(system_ref, k, p, at + VARS * a + b) * state[b] for b in range(VARS)]
-        for a in range(VARS)
-    ]
-
-
 def total(rows, first=None):
     if first is None:
-        return tuple((t[0] + t[1]) + (t[2] + t[3]) + t[4] for t in rows)
-    return tuple(((x + t[0]) + (t[1] + t[2])) + (t[3] + t[4]) for x, t in zip(first, rows))
-
-
-def get_rows(ref, k, p):
-    return [ref[k, 8 * p + a:8 * p + a + 1, :] for a in range(VARS)]
-
-
-def put_rows(ref, k, p, rows):
+        return [(t[0] + t[1]) + (t[2] + t[3]) + t[4] for t in rows]
+    return [((x + t[0]) + (t[1] + t[2])) + (t[3] + t[4]) for x, t in zip(first, rows)]
+
+
+def entry(system_ref, at, p):
+    row = 8 * (2 * at + p)
+    return system_ref[row:row + 8, :]
+
+
+def apply(system_ref, at, p, x, first=None):
+    return total(
+        [[entry(system_ref, at + VARS * a + b, p) * x[b] for b in range(VARS)] for a in range(VARS)],
+        first,
+    )
+
+
+def compose(system_ref, at, later, earlier, out_ref):
+    for c in range(VARS):
+        column = [entry(system_ref, at + VARS * b + c, earlier) for b in range(VARS)]
+        for a, x in enumerate(apply(system_ref, at, later, column)):
+            out_ref[VARS * a + c] = x
+
+
+def relay(matrix_ref, offset, offset_ref, state_ref, up):
     for a in range(VARS):
-        ref[k, 8 * p + a:8 * p + a + 1, :] = rows[a]
-
-
-def turn(state, by):
-    return tuple(pltpu.roll(x, by, 1) for x in state)
-
-
-def lower_sweep(step):
-    state = tuple(jnp.zeros((1, LANES), F32) for _ in range(VARS))
-    for group in range(GROUPS):
-        if group:
-            state = turn(state, 32)
-        state = lax.fori_loop(0, CHUNKS, functools.partial(step, group), state, unroll=True)
-
-
-def upper_sweep(step):
-    state = tuple(jnp.zeros((1, LANES), F32) for _ in range(VARS))
-    for group in reversed(range(GROUPS)):
-        if group < GROUPS - 1:
-            state = turn(state, 96)
-        state = lax.fori_loop(
-            0, CHUNKS, lambda i, x: step(group, CHUNKS - 1 - i, x), state, unroll=True
-        )
-
-
-def merged(ref):
-    shape = (CHUNKS * 16, LANES)
-    lane = lax.broadcasted_iota(jnp.int32, shape, 1) >> 5
-    row = lax.broadcasted_iota(jnp.int32, shape, 0) & 7
-    parts = [ref[group].reshape(shape) for group in range(GROUPS)]
-    out = jnp.where(lane == 0, parts[0], jnp.where(lane == 1, parts[1], jnp.where(lane == 2, parts[2], parts[3])))
-    return jnp.where(row < VARS, out, 0.0)
-
-
-def upper_pass(system_ref, lowered_ref, coupled_ref, delta_ref):
-    def upper(group, k, state):
-        for p in reversed(range(PLANES)):
-            coupled = terms(system_ref, k, p, UPPER, state)
-            put_rows(coupled_ref.at[group], k, p, total(coupled))
-            state = total(coupled, get_rows(lowered_ref.at[group], k, p))
-            put_rows(delta_ref.at[group], k, p, state)
-        return state
-
-    upper_sweep(upper)
+        offset_ref[a] = offset[a]
+    state = [jnp.zeros((1, LANES), F32) for _ in range(VARS)]
+    groups = range(GROUPS) if up else range(GROUPS - 1, -1, -1)
+    chunks = range(CHUNKS) if up else range(CHUNKS - 1, -1, -1)
+    for group in groups:
+        if group != groups[0]:
+            state = [pltpu.roll(x, 32 if up else 96, 1) for x in state]
+        for k in chunks:
+            row = slice(k, k + 1)
+            for a in range(VARS):
+                state_ref[group, a, row, :] = state[a]
+            state = total(
+                [
+                    [matrix_ref[VARS * a + b, row, :] * state[b] for b in range(VARS)]
+                    for a in range(VARS)
+                ],
+                [offset_ref[a, row, :] for a in range(VARS)],
+            )
+    lane = lax.broadcasted_iota(jnp.int32, (CHUNKS, LANES), 1) >> 5
+    out = []
+    for a in range(VARS):
+        x = state_ref[GROUPS - 1, a]
+        for group in range(GROUPS - 1):
+            x = jnp.where(lane == group, state_ref[group, a], x)
+        out.append(x)
+    return out
+
+
+def plus(x, y):
+    return [a + b for a, b in zip(x, y)]
 
 
 def face_matrix(owner_ref, count_ref):
@@ -229,70 +218,69 @@
 
 def solve_kernel(
     owner_in, count_in, in_ref, face_ref, out_ref, send_ref,
-    owner_ref, count_ref, system_ref, faces_ref, last_ref, solution_ref, residual_ref,
-    lowered_ref, coupled_ref, delta_ref, values_ref, sems,
+    owner_ref, count_ref, system_ref, lower_ref, upper_ref, offset_ref, state_ref, values_ref, sems,
 ):
+    copies = copy_in([(owner_in, owner_ref), (count_in, count_ref)], sems)
     values_ref[160:, :] = jnp.zeros((96, LANES), F32)
-    copies = copy_in([(owner_in, owner_ref), (count_in, count_ref)], sems)
     for k in range(CHUNKS):
         parts = []
         for group in range(GROUPS):
             chunk = CHUNKS * group + k
-            parts += [
-                face_rows(face_ref, chunk),
-                in_ref[32 * chunk + 16:32 * chunk + 32, :],
-            ]
-        system_ref[k] = jnp.concatenate(parts, axis=0).T
+            parts += [face_rows(face_ref, chunk), in_ref[32 * chunk + 16:32 * chunk + 32, :]]
+        system_ref[pl.ds(k, LANES, stride=CHUNKS), :] = jnp.concatenate(parts, axis=0).T
     for copy in copies:
         copy.wait()
     matrix = face_matrix(owner_ref, count_ref)
-
-    def lower_first(group, k, state):
-        for p in range(PLANES):
-            along = terms(system_ref, k, p, LOWER, state)
-            state = total(along, [entry(system_ref, k, p, SOURCE + a) for a in range(VARS)])
-            put_rows(lowered_ref.at[group], k, p, state)
-        return state
-
-    lower_sweep(lower_first)
-    upper_pass(system_ref, lowered_ref, coupled_ref, delta_ref)
-    last_ref[...] = merged(coupled_ref).reshape(last_ref.shape)
-    first = merged(delta_ref)
-    faces_ref[...] = times(first, matrix).reshape(faces_ref.shape)
-
-    def lower_second(group, k, state):
-        for p in range(PLANES):
-            along = terms(system_ref, k, p, LOWER, state)
-            faces = get_rows(faces_ref, k, p)
-            put_rows(lowered_ref.at[group], k, p, total(along, faces))
-            state = total(along, [f + e for f, e in zip(faces, get_rows(last_ref, k, p))])
-        return state
-
-    lower_sweep(lower_second)
-    upper_pass(system_ref, lowered_ref, coupled_ref, delta_ref)
-    second = merged(delta_ref)
-    solution_ref[...] = (first + second).reshape(solution_ref.shape)
-    last_ref[...] = merged(coupled_ref).reshape(last_ref.shape)
-    lane = lax.broadcasted_iota(jnp.int32, (1, LANES), 1)
-    for k in range(CHUNKS):
-        if k:
-            before = get_rows(last_ref, k - 1, 1)
-        else:
-            before = [
-                jnp.where(lane < 32, 0.0, x) for x in turn(get_rows(last_ref, CHUNKS - 1, 1), 32)
-            ]
-        put_rows(residual_ref, k, 0, total(terms(system_ref, k, 0, LOWER, before)))
-        before = get_rows(last_ref, k, 0)
-        put_rows(residual_ref, k, 1, total(terms(system_ref, k, 1, LOWER, before)))
-    residual_ref[...] = residual_ref[...] + times(second, matrix).reshape(residual_ref.shape)
-
-    for k in range(CHUNKS):
-        out_ref[k, 0:16, :] = solution_ref[k]
-        out_ref[k, 16:32, :] = residual_ref[k]
-    for k in range(CHUNKS):
-        for g in range(4):
-            at = 5 * (4 * k + g)
-            values_ref[at:at + VARS, :] = out_ref[k, 8 * g:8 * g + VARS, :]
+    lower = functools.partial(apply, system_ref, LOWER)
+    upper = functools.partial(apply, system_ref, UPPER)
+    compose(system_ref, LOWER, 1, 0, lower_ref)
+    compose(system_ref, UPPER, 0, 1, upper_ref)
+
+    def upper_sweep(lowered):
+        offset = upper(0, lowered[1], lowered[0])
+        after = relay(upper_ref, offset, offset_ref, state_ref, False)
+        coupled_1 = upper(1, after)
+        delta_1 = plus(lowered[1], coupled_1)
+        coupled_0 = upper(0, delta_1)
+        return [coupled_0, coupled_1], [plus(lowered[0], coupled_0), delta_1]
+
+    def faces_of(delta):
+        parts = times(jnp.concatenate(delta[0] + delta[1], axis=0), matrix)
+        rows = [parts[CHUNKS * i:CHUNKS * (i + 1)] for i in range(2 * VARS)]
+        return [rows[:VARS], rows[VARS:]]
+
+    source = [[entry(system_ref, SOURCE + a, p) for a in range(VARS)] for p in range(PLANES)]
+    before = relay(lower_ref, lower(1, source[0], source[1]), offset_ref, state_ref, True)
+    lowered_0 = lower(0, before, source[0])
+    lowered_1 = lower(1, lowered_0, source[1])
+    coupled, first = upper_sweep([lowered_0, lowered_1])
+
+    faces = faces_of(first)
+    joint_0 = plus(faces[0], coupled[0])
+    joint_1 = plus(faces[1], coupled[1])
+    before = relay(lower_ref, lower(1, joint_0, joint_1), offset_ref, state_ref, True)
+    along = lower(0, before)
+    lowered_1 = lower(1, plus(joint_0, along), faces[1])
+    coupled, second = upper_sweep([plus(faces[0], along), lowered_1])
+
+    faces = faces_of(second)
+    row = lax.broadcasted_iota(jnp.int32, (CHUNKS, LANES), 0)
+    lane = lax.broadcasted_iota(jnp.int32, (CHUNKS, LANES), 1)
+    previous = []
+    for x in coupled[1]:
+        x = pltpu.roll(x, 1, 0)
+        x = jnp.where(row == 0, jnp.where(lane < 32, 0.0, pltpu.roll(x, 32, 1)), x)
+        previous.append(x)
+    results = [
+        plus(first[0], second[0]),
+        plus(first[1], second[1]),
+        lower(0, previous, faces[0]),
+        lower(1, coupled[0], faces[1]),
+    ]
+    for g in range(4):
+        for a in range(VARS):
+            out_ref[pl.ds(8 * g + a, CHUNKS, stride=32), :] = results[g][a]
+            values_ref[pl.ds(5 * g + a, CHUNKS, stride=20), :] = results[g][a]
     turned = values_ref[0:LANES, :].T
     others = values_ref[LANES:2 * LANES, :].T
     lane_group = lax.broadcasted_iota(jnp.int32, (CROSS, LANES), 1) >> 5
@@ -338,7 +326,7 @@
         tiles = []
         for g in range(4):
             at = 5 * (4 * k + g)
-            tiles.append(jnp.where(returned, values_ref[at:at + 8, :], in_ref[k, 8 * g:8 * g + 8, :]))
+            tiles.append(jnp.where(returned, values_ref[at:at + 8, :], in_ref[32 * k + 8 * g:32 * k + 8 * g + 8, :]))
         for group, tile in enumerate(regroup(tiles)):
             out_ref[CHUNKS * group + k] = tile
 
@@ -409,18 +397,20 @@
     )(arrived)
     faces = lax.all_to_all(faces.reshape(CROSS * KEPT // 4, 4, LANES), "cross", 0, 0, tiled=True)
 
-    passes = pltpu.VMEM((GROUPS, CHUNKS, 16, LANES), F32)
-    chunks = pltpu.VMEM((CHUNKS, 16, LANES), F32)
+    composed = pltpu.VMEM((VARS * VARS, CHUNKS, LANES), F32)
     results, faces = pl.pallas_call(
         solve_kernel,
-        out_shape=[shape(CHUNKS, 32, LANES), shape(5 * CROSS, LANES)],
+        out_shape=[shape(CHUNKS * 32, LANES), shape(5 * CROSS, LANES)],
         in_specs=[HBM, HBM, VMEM, VMEM],
         out_specs=[VMEM, VMEM],
         scratch_shapes=[TABLE] * 2
-        + [pltpu.VMEM((CHUNKS, LANES, LANES), F32)]
-        + [chunks] * 4
-        + [passes] * 3
-        + [pltpu.VMEM((2 * LANES, LANES), F32), pltpu.SemaphoreType.DMA((2,))],
+        + [
+            pltpu.VMEM((CHUNKS * LANES, LANES), F32), composed, composed,
+            pltpu.VMEM((VARS, CHUNKS, LANES), F32),
+            pltpu.VMEM((GROUPS, VARS, CHUNKS, LANES), F32),
+            pltpu.VMEM((2 * LANES, LANES), F32),
+            pltpu.SemaphoreType.DMA((2,)),
+        ],
         compiler_params=PARAMS,
         name="solve_cells",
     )(owner, count, arrived, faces.reshape(CROSS * KEPT, LANES))

time: 91.6 us -> 90.1 us (0.984)
  Pallas kernels: 8.49 us -> 6.99 us
    pallas_call x1, Pallas kernels: 4.51 us -> 3.01 us  [local(): pl.pallas_call(solve_kernel, out_shape=[shape(CHUNKS * 32, LANES), shape(...]
where the time goes in v4:
time: 90.1 us; the launch traced here: 89.7 us
  blocking collectives  82 us (91%)
  Pallas kernels  6.99 us (8%)
    all_to_all x1, blocking collectives, local(): lax.all_to_all(faces.reshape(CROSS * KEPT // 4, 4, LANES), 'cross', 0, 0,...  26.7 us
    all_to_all x1, blocking collectives, local(): lax.all_to_all(packed.reshape(STREAM, 32, LANES), 'stream', 0, 0, tiled=T...  22.2 us
    all_to_all x1, blocking collectives, local(): lax.all_to_all(faces.reshape(5 * CROSS, 1, LANES), 'cross', 0, 0, tiled=T...  20.3 us
    all_to_all x1, blocking collectives, local(): returned = lax.all_to_all(results, 'stream', 0, 0, tiled=True)  12.8 us
    pallas_call x1, Pallas kernels, local(): pl.pallas_call(solve_kernel, out_shape=[shape(CHUNKS * 32, LANES), shape(...  3.01 us
    pallas_call x1, Pallas kernels, local(): pl.pallas_call(pack_kernel, out_shape=[shape(CELLS, LANES), jax.ShapeDtyp...  2.49 us

profile of v4, /device:TPU:1, one launch (start us, length us, event | category | flops | bytes accessed | tf_op | source)
XLA Modules:
  0.0 89.7 jit_solution(13605681136890849444)
XLA Ops:
  0.6 2.5 %pack_cells.1 = (f32[1024,128]{1,0:T(8,128)}, s32[4,256]{1,0:T(4,128)}) custom-call(s32[4,16]{1,0:T(4,128)} %bitcast.23, s32[4,16]{1,0:T(4,128)} %bitcast.31, s32[4,16]{1,0:T(4,128)} %bitcast.25, s32[4,16]{1,0:T(4,128)} %bitcast.32, s32[16]{0:T(128)} %live_in.1, f32[5,2,1024]{2,1,0:T(2,128)} %bitcast.30, f32[2,1024]{1,0:T(2,128)} %diagonal_ref.1, ...), custom_call_target="tpu_custom_call" | custom-call | tf_op jit(solution)/shard_map/pack_cells/pallas_call | solution.py:367
  3.1 22.2 %all_to_all.20 = f32[32,32,128]{2,1,0:T(8,128)S(1)} all-to-all(f32[32,32,128]{2,1,0:T(8,128)} %bitcast.27), channel_id=1, replica_groups=mesh['stream'=32,'cross'=16] {'stream'}, dimensions={0} | all-to-all | bytes 1048576 | tf_op jit(solution)/shard_map/all_to_all | solution.py:388
  25.3 0.1 take_faces.1
  25.4 0.0 copy-start.1
  25.4 0.0 copy-start.2
  25.4 26.7 %all_to_all.21 = f32[112,4,128]{2,1,0:T(4,128)S(1)} all-to-all(f32[112,4,128]{2,1,0:T(4,128)S(1)} %bitcast.20), channel_id=1, replica_groups=mesh['stream'=32,'cross'=16] {'cross'}, dimensions={0} | all-to-all | bytes 458752 | tf_op jit(solution)/shard_map/all_to_all | solution.py:398
  52.2 0.0 copy-done.1
  52.2 0.0 copy-done.2
  52.2 3.0 %solve_cells.1 = (f32[256,128]{1,0:T(8,128)S(1)}, f32[80,128]{1,0:T(8,128)S(1)}) custom-call(s32[4,16]{1,0:T(4,128)S(1)} %bitcast.24, s32[4,16]{1,0:T(4,128)S(1)} %bitcast.26, f32[1024,128]{1,0:T(8,128)S(1)} %bitcast.18, f32[448,128]{1,0:T(8,128)S(1)} %bitcast.19), custom_call_target="tpu_custom_call" | custom-call | tf_op jit(solution)/shard_map/solve_cells/pallas_call | solution.py:401
  55.2 20.3 %all_to_all.22 = f32[80,1,128]{2,1,0:T(1,128)S(1)} all-to-all(f32[80,1,128]{2,1,0:T(1,128)S(1)} %bitcast.22), channel_id=1, replica_groups=mesh['stream'=32,'cross'=16] {'cross'}, dimensions={0} | all-to-all | bytes 81920 | tf_op jit(solution)/shard_map/all_to_all | solution.py:417
  75.5 0.4 join_faces.1
  75.9 0.0 copy-start
  75.9 0.0 copy-start.3
  75.9 12.8 %all_to_all.23.in_ref = f32[32,8,128]{2,1,0:T(8,128)S(1)} all-to-all(f32[32,8,128]{2,1,0:T(8,128)S(1)} %join_faces.1), channel_id=1, replica_groups=mesh['stream'=32,'cross'=16] {'stream'}, dimensions={0} | all-to-all | bytes 262144 | tf_op jit(solution)/shard_map/all_to_all | solution.py:427
  88.7 0.0 copy-done
  88.7 0.0 copy-done.3
  88.7 1.0 %unpack_cells.1 = (f32[5,2,1024]{2,1,0:T(2,128)}, f32[5,2,1024]{2,1,0:T(2,128)}) custom-call(s32[4,256]{1,0:T(4,128)S(1)} %copy-done.3, f32[2,1024]{1,0:T(2,128)S(1)} %copy-done, f32[32,8,128]{2,1,0:T(8,128)S(1)} %all_to_all.23.in_ref), custom_call_target="tpu_custom_call" | custom-call | tf_op jit(solution)/shard_map/unpack_cells/pallas_call | solution.py:428
Async XLA Ops:
  25.4 26.8 %copy-start.1 = (s32[16,4]{0,1:T(4,128)S(1)}, s32[16,4]{0,1:T(4,128)}, u32[]{:S(2)}) copy-start(s32[16,4]{0,1:T(4,128)} %param.13) | copy-start | bytes 772
  25.4 26.7 %copy-start.2 = (s32[16,4]{0,1:T(4,128)S(1)}, s32[16,4]{0,1:T(4,128)}, u32[]{:S(2)}) copy-start(s32[16,4]{0,1:T(4,128)} %param.15) | copy-start | bytes 772
  75.9 12.8 %copy-start = (f32[2,1024]{1,0:T(2,128)S(1)}, f32[2,1024]{1,0:T(2,128)}, u32[]{:S(2)}) copy-start(f32[2,1024]{1,0:T(2,128)} %diagonal_ref.1) | copy-start | bytes 24580
  75.9 12.8 %copy-start.3 = (s32[4,256]{1,0:T(4,128)S(1)}, s32[4,256]{1,0:T(4,128)}, u32[]{:S(2)}) copy-start(s32[4,256]{1,0:T(4,128)} %get-tuple-element.8.slots_ref) | copy-start | bytes 12292

commit v5 on v4

--- a/solution.py
+++ b/solution.py
@@ -32,7 +32,6 @@
 SMEM = pl.BlockSpec(memory_space=pltpu.SMEM)
 VMEM = pl.BlockSpec(memory_space=pltpu.VMEM)
 PARAMS = pltpu.CompilerParams(vmem_limit_bytes=24 * 1024 * 1024)
-WIDE = pltpu.CompilerParams(vmem_limit_bytes=62 * 1024 * 1024)
 TABLE = pltpu.SMEM((LINKS, CROSS), jnp.int32)
 
 
@@ -77,9 +76,9 @@
 
 def pack_kernel(
     owner_in, start_in, count_in, flip_in, live_in, rhs_in, diagonal_in, lower_in, upper_in,
-    out_ref, slots_ref,
+    out_ref, matrix_ref,
     owner_ref, start_ref, count_ref, flip_ref, live_ref, rhs_ref, diagonal_ref, lower_ref, upper_ref,
-    rows_ref, matrix_ref, sems,
+    rows_ref, sems,
 ):
     copies = copy_in(
         [
@@ -94,9 +93,7 @@
     for copy in copies[:5]:
         copy.wait()
     for link in range(LINKS):
-        slots = slots_of(own, link, owner_ref, start_ref, count_ref, flip_ref)
-        slots_ref[link:link + 1, :] = slots
-        matrix_ref[link] = onehot(slots)
+        matrix_ref[link] = onehot(slots_of(own, link, owner_ref, start_ref, count_ref, flip_ref))
     for copy in copies[5:]:
         copy.wait()
     cell = lax.broadcasted_iota(jnp.int32, (PLANES, CELLS), 1)
@@ -331,14 +328,14 @@
             out_ref[CHUNKS * group + k] = tile
 
 
-def unpack_kernel(slots_ref, diagonal_ref, in_ref, solution_ref, residual_ref, rows_ref):
+def unpack_kernel(matrix_ref, diagonal_ref, in_ref, solution_ref, residual_ref, rows_ref):
     for column in range(8):
         tiles = regroup([in_ref[4 * column + e] for e in range(4)])
         for g, tile in enumerate(tiles):
             rows_ref[8 * g:8 * g + 8, LANES * column:LANES * (column + 1)] = tile
     for link in range(LINKS):
         window = slice(link * WINDOW, (link + 1) * WINDOW)
-        cells = times(rows_ref[:, window], onehot(slots_ref[link:link + 1, :]))
+        cells = times(rows_ref[:, window], matrix_ref[link])
         for p in range(PLANES):
             residual = cells[16 + 8 * p:16 + 8 * p + VARS] * diagonal_ref[p:p + 1, window]
             for a in range(VARS):
@@ -364,26 +361,31 @@
     owner, start, count, flip = face_owner.T, face_start.T, face_count.T, face_flip.T
     transfer = pltpu.VMEM((VARS, VARS, PLANES, CELLS), F32)
     planes = pltpu.VMEM((PLANES, CELLS), F32)
-    packed, slots = pl.pallas_call(
+    in_hbm = functools.partial(pltpu.with_memory_space_constraint, memory_space=pltpu.HBM)
+    packed, matrix = pl.pallas_call(
         pack_kernel,
-        out_shape=[shape(CELLS, LANES), jax.ShapeDtypeStruct((LINKS, WINDOW), jnp.int32)],
+        out_shape=[shape(CELLS, LANES), jax.ShapeDtypeStruct((LINKS, WINDOW, WINDOW), BF16)],
         in_specs=[HBM] * 9,
         out_specs=[VMEM] * 2,
         scratch_shapes=[TABLE] * 4
         + [
             pltpu.SMEM((CROSS,), jnp.int32), pltpu.VMEM((VARS, PLANES, CELLS), F32), planes,
-            transfer, transfer, pltpu.VMEM((LANES, CELLS), F32),
-            pltpu.VMEM((LINKS, WINDOW, WINDOW), BF16), pltpu.SemaphoreType.DMA((9,)),
+            transfer, transfer, pltpu.VMEM((LANES, CELLS), F32), pltpu.SemaphoreType.DMA((9,)),
         ],
-        compiler_params=WIDE,
+        compiler_params=PARAMS,
         name="pack_cells",
     )(
-        owner, start, count, flip,
-        block_cells,
-        rhs.transpose(1, 0, 2),
-        diagonal,
-        lower_transfer.transpose(1, 2, 0, 3),
-        upper_transfer.transpose(1, 2, 0, 3),
+        *[
+            in_hbm(x)
+            for x in (
+                owner, start, count, flip,
+                block_cells,
+                rhs.transpose(1, 0, 2),
+                diagonal,
+                lower_transfer.transpose(1, 2, 0, 3),
+                upper_transfer.transpose(1, 2, 0, 3),
+            )
+        ]
     )
     arrived = lax.all_to_all(packed.reshape(STREAM, 32, LANES), "stream", 0, 0, tiled=True)
     arrived = arrived.reshape(CELLS, LANES)
@@ -433,7 +435,7 @@
         scratch_shapes=[pltpu.VMEM((32, CELLS), F32)],
         compiler_params=PARAMS,
         name="unpack_cells",
-    )(slots, diagonal, returned)
+    )(matrix, diagonal, returned)
     return tuple(x.transpose(1, 0, 2) for x in outs)
 
 

time: 90.1 us -> 89 us (0.988)
    all_to_all x1, blocking collectives: 22.2 us -> 21.3 us  [local(): lax.all_to_all(packed.reshape(STREAM, 32, LANES), 'stream', 0, 0, tiled=T...]
where the time goes in v5:
time: 89 us; the launch traced here: 88.7 us
  blocking collectives  81.8 us (92%)
  Pallas kernels  6.16 us (7%)
    all_to_all x1, blocking collectives, local(): lax.all_to_all(faces.reshape(CROSS * KEPT // 4, 4, LANES), 'cross', 0, 0,...  27.4 us
    all_to_all x1, blocking collectives, local(): lax.all_to_all(packed.reshape(STREAM, 32, LANES), 'stream', 0, 0, tiled=T...  21.3 us
    all_to_all x1, blocking collectives, local(): lax.all_to_all(faces.reshape(5 * CROSS, 1, LANES), 'cross', 0, 0, tiled=T...  20.3 us
    all_to_all x1, blocking collectives, local(): returned = lax.all_to_all(results, 'stream', 0, 0, tiled=True)  12.8 us
    pallas_call x1, Pallas kernels, local(): pl.pallas_call(solve_kernel, out_shape=[shape(CHUNKS * 32, LANES), shape(...  3.01 us

profile of v5, /device:TPU:1, one launch (start us, length us, event | category | flops | bytes accessed | tf_op | source)
XLA Modules:
  0.0 88.7 jit_solution(1389563940553905512)
XLA Ops:
  0.6 1.7 %pack_cells.1 = (f32[1024,128]{1,0:T(8,128)S(1)}, bf16[4,256,256]{2,1,0:T(8,128)(2,1)S(1)}) custom-call(s32[4,16]{1,0:T(4,128)} %bitcast.24, s32[4,16]{1,0:T(4,128)} %bitcast.31, s32[4,16]{1,0:T(4,128)} %bitcast.26, s32[4,16]{1,0:T(4,128)} %bitcast.32, s32[16]{0:T(128)} %live_in.1, f32[5,2,1024]{2,1,0:T(2,128)} %bitcast.30, f32[2,1024]{1,0:T(2,128)} %diagonal_ref.1, ...), custom_call_target="tpu_custom_call" | custom-call | tf_op jit(solution)/shard_map/pack_cells/pallas_call | solution.py:365
  2.3 21.3 %all_to_all.20 = f32[32,32,128]{2,1,0:T(8,128)S(1)} all-to-all(f32[32,32,128]{2,1,0:T(8,128)S(1)} %bitcast.21), channel_id=1, replica_groups=mesh['stream'=32,'cross'=16] {'stream'}, dimensions={0} | all-to-all | bytes 1048576 | tf_op jit(solution)/shard_map/all_to_all | solution.py:390
  23.6 0.1 take_faces.1
  23.7 0.0 copy-start.1
  23.7 0.0 copy-start.2
  23.7 27.4 %all_to_all.21 = f32[112,4,128]{2,1,0:T(4,128)S(1)} all-to-all(f32[112,4,128]{2,1,0:T(4,128)S(1)} %bitcast.20), channel_id=1, replica_groups=mesh['stream'=32,'cross'=16] {'cross'}, dimensions={0} | all-to-all | bytes 458752 | tf_op jit(solution)/shard_map/all_to_all | solution.py:400
  51.1 0.0 copy-done.1
  51.1 0.0 copy-done.2
  51.1 3.0 %solve_cells.1 = (f32[256,128]{1,0:T(8,128)S(1)}, f32[80,128]{1,0:T(8,128)S(1)}) custom-call(s32[4,16]{1,0:T(4,128)S(1)} %bitcast.25, s32[4,16]{1,0:T(4,128)S(1)} %bitcast.27, f32[1024,128]{1,0:T(8,128)S(1)} %bitcast.18, f32[448,128]{1,0:T(8,128)S(1)} %bitcast.19), custom_call_target="tpu_custom_call" | custom-call | tf_op jit(solution)/shard_map/solve_cells/pallas_call | solution.py:403
  54.2 20.3 %all_to_all.22 = f32[80,1,128]{2,1,0:T(1,128)S(1)} all-to-all(f32[80,1,128]{2,1,0:T(1,128)S(1)} %bitcast.23), channel_id=1, replica_groups=mesh['stream'=32,'cross'=16] {'cross'}, dimensions={0} | all-to-all | bytes 81920 | tf_op jit(solution)/shard_map/all_to_all | solution.py:419
  74.5 0.4 join_faces.1
  74.9 0.0 copy-start
  74.9 12.8 %all_to_all.23.in_ref = f32[32,8,128]{2,1,0:T(8,128)S(1)} all-to-all(f32[32,8,128]{2,1,0:T(8,128)S(1)} %join_faces.1), channel_id=1, replica_groups=mesh['stream'=32,'cross'=16] {'stream'}, dimensions={0} | all-to-all | bytes 262144 | tf_op jit(solution)/shard_map/all_to_all | solution.py:429
  87.7 0.0 copy-done
  87.7 1.0 %unpack_cells.1 = (f32[5,2,1024]{2,1,0:T(2,128)}, f32[5,2,1024]{2,1,0:T(2,128)}) custom-call(bf16[4,256,256]{2,1,0:T(8,128)(2,1)S(1)} %get-tuple-element.8.matrix_ref, f32[2,1024]{1,0:T(2,128)S(1)} %copy-done, f32[32,8,128]{2,1,0:T(8,128)S(1)} %all_to_all.23.in_ref), custom_call_target="tpu_custom_call" | custom-call | tf_op jit(solution)/shard_map/unpack_cells/pallas_call | solution.py:430
Async XLA Ops:
  23.7 27.4 %copy-start.1 = (s32[16,4]{0,1:T(4,128)S(1)}, s32[16,4]{0,1:T(4,128)}, u32[]{:S(2)}) copy-start(s32[16,4]{0,1:T(4,128)} %param.13) | copy-start | bytes 772
  23.7 27.4 %copy-start.2 = (s32[16,4]{0,1:T(4,128)S(1)}, s32[16,4]{0,1:T(4,128)}, u32[]{:S(2)}) copy-start(s32[16,4]{0,1:T(4,128)} %param.15) | copy-start | bytes 772
  74.9 12.8 %copy-start = (f32[2,1024]{1,0:T(2,128)S(1)}, f32[2,1024]{1,0:T(2,128)}, u32[]{:S(2)}) copy-start(f32[2,1024]{1,0:T(2,128)} %diagonal_ref.1) | copy-start | bytes 24580

commit v6 on v5

--- a/solution.py
+++ b/solution.py
@@ -199,31 +199,34 @@
         out_ref[pl.ds(row, CROSS, stride=KEPT), :] = jnp.where(lane < ROWS, own, spare)
 
 
-def face_rows(face_ref, chunk):
-    if chunk < KEPT:
-        return face_ref[pl.ds(chunk, CROSS, stride=KEPT), :]
+def gather_faces(face_ref, rows_ref):
     piece_of = lax.broadcasted_iota(jnp.int32, (CROSS, LANES), 1) >> 4
-    out = jnp.zeros((CROSS, LANES), F32)
-    for piece in range(PIECES):
-        row = PIECES * (chunk - KEPT) + piece
-        moved = pltpu.roll(
-            face_ref[pl.ds(row, CROSS, stride=KEPT), :], LANES - ROWS + 16 * piece, 1
-        )
-        out = jnp.where(piece_of == piece, moved, out)
-    return out
+    for chunk in range(KEPT, STREAM):
+        last = jnp.zeros((CROSS, LANES), F32)
+        for piece in range(PIECES):
+            row = PIECES * (chunk - KEPT) + piece
+            found = face_ref[pl.ds(row, CROSS, stride=KEPT), :]
+            rows_ref[CROSS * row:CROSS * (row + 1), :] = found
+            moved = pltpu.roll(found, LANES - ROWS + 16 * piece, 1)
+            last = jnp.where(piece_of == piece, moved, last)
+        rows_ref[CROSS * chunk:CROSS * (chunk + 1), :] = last
 
 
 def solve_kernel(
     owner_in, count_in, in_ref, face_ref, out_ref, send_ref,
-    owner_ref, count_ref, system_ref, lower_ref, upper_ref, offset_ref, state_ref, values_ref, sems,
+    owner_ref, count_ref, rows_ref, system_ref, lower_ref, upper_ref, offset_ref, state_ref, values_ref, sems,
 ):
     copies = copy_in([(owner_in, owner_ref), (count_in, count_ref)], sems)
     values_ref[160:, :] = jnp.zeros((96, LANES), F32)
+    gather_faces(face_ref, rows_ref)
     for k in range(CHUNKS):
         parts = []
         for group in range(GROUPS):
             chunk = CHUNKS * group + k
-            parts += [face_rows(face_ref, chunk), in_ref[32 * chunk + 16:32 * chunk + 32, :]]
+            parts += [
+                rows_ref[CROSS * chunk:CROSS * (chunk + 1), :],
+                in_ref[32 * chunk + 16:32 * chunk + 32, :],
+            ]
         system_ref[pl.ds(k, LANES, stride=CHUNKS), :] = jnp.concatenate(parts, axis=0).T
     for copy in copies:
         copy.wait()
@@ -276,8 +279,9 @@
     ]
     for g in range(4):
         for a in range(VARS):
-            out_ref[pl.ds(8 * g + a, CHUNKS, stride=32), :] = results[g][a]
-            values_ref[pl.ds(5 * g + a, CHUNKS, stride=20), :] = results[g][a]
+            at = CHUNKS * (VARS * g + a)
+            out_ref[at:at + CHUNKS, :] = results[g][a]
+            values_ref[at:at + CHUNKS, :] = results[g][a]
     turned = values_ref[0:LANES, :].T
     others = values_ref[LANES:2 * LANES, :].T
     lane_group = lax.broadcasted_iota(jnp.int32, (CROSS, LANES), 1) >> 5
@@ -319,20 +323,23 @@
         others += [pltpu.roll(fifth, (LANES - 32 * group) % LANES, 1) if group else fifth, blank]
     values_ref[0:LANES, :] = jnp.concatenate(parts, axis=0).T
     values_ref[LANES:2 * LANES, :] = jnp.concatenate(others, axis=0).T
-    for k in range(CHUNKS):
+    for a in range(VARS):
         tiles = []
         for g in range(4):
-            at = 5 * (4 * k + g)
-            tiles.append(jnp.where(returned, values_ref[at:at + 8, :], in_ref[32 * k + 8 * g:32 * k + 8 * g + 8, :]))
+            at = CHUNKS * (VARS * g + a)
+            rows = slice(at, at + CHUNKS)
+            tiles.append(jnp.where(returned, values_ref[rows, :], in_ref[rows, :]))
         for group, tile in enumerate(regroup(tiles)):
-            out_ref[CHUNKS * group + k] = tile
+            out_ref[pl.ds(VARS * CHUNKS * group + a, CHUNKS, stride=VARS), :] = tile
 
 
 def unpack_kernel(matrix_ref, diagonal_ref, in_ref, solution_ref, residual_ref, rows_ref):
     for column in range(8):
-        tiles = regroup([in_ref[4 * column + e] for e in range(4)])
+        tiles = regroup(
+            [in_ref[VARS * (4 * column + e):VARS * (4 * column + e + 1), :] for e in range(4)]
+        )
         for g, tile in enumerate(tiles):
-            rows_ref[8 * g:8 * g + 8, LANES * column:LANES * (column + 1)] = tile
+            rows_ref[8 * g:8 * g + VARS, LANES * column:LANES * (column + 1)] = tile
     for link in range(LINKS):
         window = slice(link * WINDOW, (link + 1) * WINDOW)
         cells = times(rows_ref[:, window], matrix_ref[link])
@@ -402,11 +409,12 @@
     composed = pltpu.VMEM((VARS * VARS, CHUNKS, LANES), F32)
     results, faces = pl.pallas_call(
         solve_kernel,
-        out_shape=[shape(CHUNKS * 32, LANES), shape(5 * CROSS, LANES)],
+        out_shape=[shape(CHUNKS * 4 * VARS, LANES), shape(5 * CROSS, LANES)],
         in_specs=[HBM, HBM, VMEM, VMEM],
         out_specs=[VMEM, VMEM],
         scratch_shapes=[TABLE] * 2
         + [
+            pltpu.VMEM((CELLS // 2, LANES), F32),
             pltpu.VMEM((CHUNKS * LANES, LANES), F32), composed, composed,
             pltpu.VMEM((VARS, CHUNKS, LANES), F32),
             pltpu.VMEM((GROUPS, VARS, CHUNKS, LANES), F32),
@@ -419,14 +427,16 @@
     faces = lax.all_to_all(faces.reshape(5 * CROSS, 1, LANES), "cross", 0, 0, tiled=True)
     results = pl.pallas_call(
         join_kernel,
-        out_shape=shape(STREAM, 8, LANES),
+        out_shape=shape(STREAM * VARS, LANES),
         in_specs=[VMEM, VMEM],
         out_specs=VMEM,
         scratch_shapes=[pltpu.VMEM((2 * LANES, LANES), F32)],
         compiler_params=PARAMS,
         name="join_faces",
     )(results, faces.reshape(5 * CROSS, LANES))
-    returned = lax.all_to_all(results, "stream", 0, 0, tiled=True)
+    returned = lax.all_to_all(
+        results.reshape(STREAM * VARS, 1, LANES), "stream", 0, 0, tiled=True
+    )
     outs = pl.pallas_call(
         unpack_kernel,
         out_shape=[shape(VARS, PLANES, CELLS)] * 2,
@@ -435,7 +445,7 @@
         scratch_shapes=[pltpu.VMEM((32, CELLS), F32)],
         compiler_params=PARAMS,
         name="unpack_cells",
-    )(matrix, diagonal, returned)
+    )(matrix, diagonal, returned.reshape(STREAM * VARS, LANES))
     return tuple(x.transpose(1, 0, 2) for x in outs)
 
 

time: 89 us -> 88.8 us (level)
  no operation moved by 1% of the time
where the time goes in v6:
time: 88.8 us; the launch traced here: 88.5 us
  blocking collectives  81.5 us (92%)
  Pallas kernels  6.25 us (7%)
    all_to_all x1, blocking collectives, local(): lax.all_to_all(faces.reshape(CROSS * KEPT // 4, 4, LANES), 'cross', 0, 0,...  27.4 us
    all_to_all x1, blocking collectives, local(): lax.all_to_all(packed.reshape(STREAM, 32, LANES), 'stream', 0, 0, tiled=T...  21.3 us
    all_to_all x1, blocking collectives, local(): lax.all_to_all(faces.reshape(5 * CROSS, 1, LANES), 'cross', 0, 0, tiled=T...  20.3 us
    all_to_all x1, blocking collectives, local(): lax.all_to_all(results.reshape(STREAM * VARS, 1, LANES), 'stream', 0, 0,...  12.5 us
    pallas_call x1, Pallas kernels, local(): pl.pallas_call(solve_kernel, out_shape=[shape(CHUNKS * 4 * VARS, LANES),...  3.11 us

profile of v6, /device:TPU:1, one launch (start us, length us, event | category | flops | bytes accessed | tf_op | source)
XLA Modules:
  0.0 88.5 jit_solution(13626414538484841008)
XLA Ops:
  0.6 1.7 %pack_cells.1 = (f32[1024,128]{1,0:T(8,128)S(1)}, bf16[4,256,256]{2,1,0:T(8,128)(2,1)S(1)}) custom-call(s32[4,16]{1,0:T(4,128)} %bitcast.30, s32[4,16]{1,0:T(4,128)} %bitcast.37, s32[4,16]{1,0:T(4,128)} %bitcast.32, s32[4,16]{1,0:T(4,128)} %bitcast.38, s32[16]{0:T(128)} %live_in.1, f32[5,2,1024]{2,1,0:T(2,128)} %bitcast.36, f32[2,1024]{1,0:T(2,128)} %diagonal_ref.1, ...), custom_call_target="tpu_custom_call" | custom-call | tf_op jit(solution)/shard_map/pack_cells/pallas_call | solution.py:372
  2.3 21.3 %all_to_all.20 = f32[32,32,128]{2,1,0:T(8,128)S(1)} all-to-all(f32[32,32,128]{2,1,0:T(8,128)S(1)} %bitcast.25), channel_id=1, replica_groups=mesh['stream'=32,'cross'=16] {'stream'}, dimensions={0} | all-to-all | bytes 1048576 | tf_op jit(solution)/shard_map/all_to_all | solution.py:397
  23.6 0.1 take_faces.1
  23.7 0.0 copy-start.1
  23.7 0.0 copy-start.2
  23.7 27.4 %all_to_all.21 = f32[112,4,128]{2,1,0:T(4,128)S(1)} all-to-all(f32[112,4,128]{2,1,0:T(4,128)S(1)} %bitcast.24), channel_id=1, replica_groups=mesh['stream'=32,'cross'=16] {'cross'}, dimensions={0} | all-to-all | bytes 458752 | tf_op jit(solution)/shard_map/all_to_all | solution.py:407
  51.1 0.0 copy-done.1
  51.1 0.0 copy-done.2
  51.1 3.1 %solve_cells.1 = (f32[160,128]{1,0:T(8,128)S(1)}, f32[80,128]{1,0:T(8,128)S(1)}) custom-call(s32[4,16]{1,0:T(4,128)S(1)} %bitcast.31, s32[4,16]{1,0:T(4,128)S(1)} %bitcast.33, f32[1024,128]{1,0:T(8,128)S(1)} %bitcast.22, f32[448,128]{1,0:T(8,128)S(1)} %bitcast.23), custom_call_target="tpu_custom_call" | custom-call | tf_op jit(solution)/shard_map/solve_cells/pallas_call | solution.py:410
  54.3 20.3 %all_to_all.22 = f32[80,1,128]{2,1,0:T(1,128)S(1)} all-to-all(f32[80,1,128]{2,1,0:T(1,128)S(1)} %bitcast.29), channel_id=1, replica_groups=mesh['stream'=32,'cross'=16] {'cross'}, dimensions={0} | all-to-all | bytes 81920 | tf_op jit(solution)/shard_map/all_to_all | solution.py:427
  74.6 0.3 join_faces.1
  74.9 0.0 copy-start
  74.9 12.5 %all_to_all.23 = f32[160,1,128]{2,1,0:T(1,128)S(1)} all-to-all(f32[160,1,128]{2,1,0:T(1,128)S(1)} %bitcast.27), channel_id=1, replica_groups=mesh['stream'=32,'cross'=16] {'stream'}, dimensions={0} | all-to-all | bytes 163840 | tf_op jit(solution)/shard_map/all_to_all | solution.py:437
  87.5 0.0 copy-done
  87.5 1.0 %unpack_cells.1 = (f32[5,2,1024]{2,1,0:T(2,128)}, f32[5,2,1024]{2,1,0:T(2,128)}) custom-call(bf16[4,256,256]{2,1,0:T(8,128)(2,1)S(1)} %get-tuple-element.8.matrix_ref, f32[2,1024]{1,0:T(2,128)S(1)} %copy-done, f32[160,128]{1,0:T(8,128)S(1)} %bitcast.26), custom_call_target="tpu_custom_call" | custom-call | tf_op jit(solution)/shard_map/unpack_cells/pallas_call | solution.py:440
Async XLA Ops:
  23.7 27.4 %copy-start.1 = (s32[16,4]{0,1:T(4,128)S(1)}, s32[16,4]{0,1:T(4,128)}, u32[]{:S(2)}) copy-start(s32[16,4]{0,1:T(4,128)} %param.13) | copy-start | bytes 772
  23.7 27.4 %copy-start.2 = (s32[16,4]{0,1:T(4,128)S(1)}, s32[16,4]{0,1:T(4,128)}, u32[]{:S(2)}) copy-start(s32[16,4]{0,1:T(4,128)} %param.15) | copy-start | bytes 772
  74.9 12.5 %copy-start = (f32[2,1024]{1,0:T(2,128)S(1)}, f32[2,1024]{1,0:T(2,128)}, u32[]{:S(2)}) copy-start(f32[2,1024]{1,0:T(2,128)} %diagonal_ref.1) | copy-start | bytes 24580

commit v7 on v6

--- a/solution.py
+++ b/solution.py
@@ -23,6 +23,7 @@
 UPPER = 25
 SOURCE = 50
 ROWS = 110
+ORDER = list(range(0, CROSS, 2)) + list(range(CROSS - 1, 0, -2))
 KEPT = 28
 PIECES = 7
 
@@ -176,15 +177,21 @@
     return [a + b for a, b in zip(x, y)]
 
 
+def rank_of(block):
+    return jnp.where((block & 1) == 0, block >> 1, CROSS - 1 - (block >> 1))
+
+
 def face_matrix(owner_ref, count_ref):
     position = lax.axis_index("stream")
     link = position >> 3
-    slot = ((position & 7) << 4) + lax.axis_index("cross")
+    slot = ((position & 7) << 4) + rank_of(lax.axis_index("cross"))
     lane = lax.broadcasted_iota(jnp.int32, (1, LANES), 1)
     source = jnp.full((1, LANES), -1, jnp.int32)
-    for block in range(CROSS):
-        taken = jnp.where(slot < count_ref[link, block], owner_ref[link, block], -LANES)
-        source = jnp.where((lane & 31) == block, (lane & 96) + taken, source)
+    for rank, block in enumerate(ORDER):
+        taken = jnp.where(
+            slot < count_ref[link, block], rank_of(owner_ref[link, block]), -LANES
+        )
+        source = jnp.where((lane & 31) == rank, (lane & 96) + taken, source)
     rows = lax.broadcasted_iota(jnp.int32, (LANES, LANES), 0)
     return jnp.where(rows == source, FACE_WEIGHT, 0.0).astype(BF16)
 
@@ -404,7 +411,7 @@
         compiler_params=PARAMS,
         name="take_faces",
     )(arrived)
-    faces = lax.all_to_all(faces.reshape(CROSS * KEPT // 4, 4, LANES), "cross", 0, 0, tiled=True)
+    faces = lax.all_to_all(faces.reshape(CROSS * KEPT // 4, 4, LANES), "cross", 0, 0, axis_index_groups=[ORDER], tiled=True)
 
     composed = pltpu.VMEM((VARS * VARS, CHUNKS, LANES), F32)
     results, faces = pl.pallas_call(
@@ -424,7 +431,7 @@
         compiler_params=PARAMS,
         name="solve_cells",
     )(owner, count, arrived, faces.reshape(CROSS * KEPT, LANES))
-    faces = lax.all_to_all(faces.reshape(5 * CROSS, 1, LANES), "cross", 0, 0, tiled=True)
+    faces = lax.all_to_all(faces.reshape(5 * CROSS, 1, LANES), "cross", 0, 0, axis_index_groups=[ORDER], tiled=True)
     results = pl.pallas_call(
         join_kernel,
         out_shape=shape(STREAM * VARS, LANES),

time: 88.8 us -> 88.8 us (level)
  no operation moved by 1% of the time
where the time goes in v7:
time: 88.8 us; the launch traced here: 88.5 us
  blocking collectives  81.6 us (92%)
  Pallas kernels  6.25 us (7%)
    all_to_all x1, blocking collectives, local(): lax.all_to_all(faces.reshape(CROSS * KEPT // 4, 4, LANES), 'cross', 0, 0,...  27.6 us
    all_to_all x1, blocking collectives, local(): lax.all_to_all(packed.reshape(STREAM, 32, LANES), 'stream', 0, 0, tiled=T...  21.3 us
    all_to_all x1, blocking collectives, local(): lax.all_to_all(faces.reshape(5 * CROSS, 1, LANES), 'cross', 0, 0, axis_in...  20.2 us
    all_to_all x1, blocking collectives, local(): lax.all_to_all(results.reshape(STREAM * VARS, 1, LANES), 'stream', 0, 0,...  12.6 us
    pallas_call x1, Pallas kernels, local(): pl.pallas_call(solve_kernel, out_shape=[shape(CHUNKS * 4 * VARS, LANES),...  3.11 us

profile of v7, /device:TPU:1, one launch (start us, length us, event | category | flops | bytes accessed | tf_op | source)
XLA Modules:
  0.0 88.5 jit_solution(10256256758173723046)
XLA Ops:
  0.6 1.7 %pack_cells.1 = (f32[1024,128]{1,0:T(8,128)S(1)}, bf16[4,256,256]{2,1,0:T(8,128)(2,1)S(1)}) custom-call(s32[4,16]{1,0:T(4,128)} %bitcast.30, s32[4,16]{1,0:T(4,128)} %bitcast.37, s32[4,16]{1,0:T(4,128)} %bitcast.32, s32[4,16]{1,0:T(4,128)} %bitcast.38, s32[16]{0:T(128)} %live_in.1, f32[5,2,1024]{2,1,0:T(2,128)} %bitcast.36, f32[2,1024]{1,0:T(2,128)} %diagonal_ref.1, ...), custom_call_target="tpu_custom_call" | custom-call | tf_op jit(solution)/shard_map/pack_cells/pallas_call | solution.py:379
  2.3 21.3 %all_to_all.20 = f32[32,32,128]{2,1,0:T(8,128)S(1)} all-to-all(f32[32,32,128]{2,1,0:T(8,128)S(1)} %bitcast.25), channel_id=1, replica_groups=mesh['stream'=32,'cross'=16] {'stream'}, dimensions={0} | all-to-all | bytes 1048576 | tf_op jit(solution)/shard_map/all_to_all | solution.py:404
  23.6 0.1 take_faces.1
  23.7 0.0 copy-start.1
  23.7 0.0 copy-start.2
  23.7 27.6 %all_to_all.21 = f32[112,4,128]{2,1,0:T(4,128)S(1)} all-to-all(f32[112,4,128]{2,1,0:T(4,128)S(1)} %bitcast.24), channel_id=1, replica_groups={{0,2,4,6,8,10,12,14,15,13,11,9,7,5,3,1},{16,18,20,22,24,26,28,30,31,29,..., dimensions={0} | all-to-all | bytes 458752 | tf_op jit(solution)/shard_map/all_to_all | solution.py:414
  51.3 0.0 copy-done.1
  51.3 0.0 copy-done.2
  51.3 3.1 %solve_cells.1 = (f32[160,128]{1,0:T(8,128)S(1)}, f32[80,128]{1,0:T(8,128)S(1)}) custom-call(s32[4,16]{1,0:T(4,128)S(1)} %bitcast.31, s32[4,16]{1,0:T(4,128)S(1)} %bitcast.33, f32[1024,128]{1,0:T(8,128)S(1)} %bitcast.22, f32[448,128]{1,0:T(8,128)S(1)} %bitcast.23), custom_call_target="tpu_custom_call" | custom-call | tf_op jit(solution)/shard_map/solve_cells/pallas_call | solution.py:417
  54.4 20.2 %all_to_all.22 = f32[80,1,128]{2,1,0:T(1,128)S(1)} all-to-all(f32[80,1,128]{2,1,0:T(1,128)S(1)} %bitcast.29), channel_id=1, replica_groups={{0,2,4,6,8,10,12,14,15,13,11,9,7,5,3,1},{16,18,20,22,24,26,28,30,31,29,..., dimensions={0} | all-to-all | bytes 81920 | tf_op jit(solution)/shard_map/all_to_all | solution.py:434
  74.6 0.3 join_faces.1
  74.9 0.0 copy-start
  74.9 12.6 %all_to_all.23 = f32[160,1,128]{2,1,0:T(1,128)S(1)} all-to-all(f32[160,1,128]{2,1,0:T(1,128)S(1)} %bitcast.27), channel_id=1, replica_groups=mesh['stream'=32,'cross'=16] {'stream'}, dimensions={0} | all-to-all | bytes 163840 | tf_op jit(solution)/shard_map/all_to_all | solution.py:444
  87.5 0.0 copy-done
  87.5 1.0 %unpack_cells.1 = (f32[5,2,1024]{2,1,0:T(2,128)}, f32[5,2,1024]{2,1,0:T(2,128)}) custom-call(bf16[4,256,256]{2,1,0:T(8,128)(2,1)S(1)} %get-tuple-element.8.matrix_ref, f32[2,1024]{1,0:T(2,128)S(1)} %copy-done, f32[160,128]{1,0:T(8,128)S(1)} %bitcast.26), custom_call_target="tpu_custom_call" | custom-call | tf_op jit(solution)/shard_map/unpack_cells/pallas_call | solution.py:447
Async XLA Ops:
  23.7 27.6 %copy-start.1 = (s32[16,4]{0,1:T(4,128)S(1)}, s32[16,4]{0,1:T(4,128)}, u32[]{:S(2)}) copy-start(s32[16,4]{0,1:T(4,128)} %param.13) | copy-start | bytes 772
  23.7 27.6 %copy-start.2 = (s32[16,4]{0,1:T(4,128)S(1)}, s32[16,4]{0,1:T(4,128)}, u32[]{:S(2)}) copy-start(s32[16,4]{0,1:T(4,128)} %param.15) | copy-start | bytes 772
  74.9 12.6 %copy-start = (f32[2,1024]{1,0:T(2,128)S(1)}, f32[2,1024]{1,0:T(2,128)}, u32[]{:S(2)}) copy-start(f32[2,1024]{1,0:T(2,128)} %diagonal_ref.1) | copy-start | bytes 24580

commit v8 on v7

--- a/solution.py
+++ b/solution.py
@@ -23,7 +23,18 @@
 UPPER = 25
 SOURCE = 50
 ROWS = 110
-ORDER = list(range(0, CROSS, 2)) + list(range(CROSS - 1, 0, -2))
+ORDER = [z for i in range(CROSS // 2) for z in (i, CROSS - 1 - i)]
+ENDS = (0, 3, 1, 2)
+CORNERS = sorted(
+    range(STREAM),
+    key=lambda s: (
+        ENDS.index(s // 8) // 2 + ENDS.index(s // 2 % 4) // 2,
+        ENDS.index(s // 8) ^ ENDS.index(s // 2 % 4),
+        ENDS.index(s // 8),
+        s % 2,
+    ),
+)
+PLACE = [CORNERS.index(s) for s in range(STREAM)]
 KEPT = 28
 PIECES = 7
 
@@ -113,9 +124,10 @@
             (((1,), (1,)), ((), ())),
             preferred_element_type=F32,
         )
-        out_ref[link * WINDOW:(link + 1) * WINDOW, :] = (
-            parts[:, 2 * LANES:] + parts[:, LANES:2 * LANES]
-        ) + parts[:, :LANES]
+        rows = (parts[:, 2 * LANES:] + parts[:, LANES:2 * LANES]) + parts[:, :LANES]
+        for e in range(8):
+            first = 32 * PLACE[8 * link + e]
+            out_ref[first:first + 32, :] = rows[32 * e:32 * e + 32]
 
 
 def total(rows, first=None):
@@ -178,7 +190,7 @@
 
 
 def rank_of(block):
-    return jnp.where((block & 1) == 0, block >> 1, CROSS - 1 - (block >> 1))
+    return jnp.where(block < CROSS // 2, 2 * block, 2 * (CROSS - 1 - block) + 1)
 
 
 def face_matrix(owner_ref, count_ref):
@@ -200,9 +212,9 @@
     lane = lax.broadcasted_iota(jnp.int32, (CROSS, LANES), 1)
     for row in range(KEPT):
         piece = row % PIECES
-        first = 32 * (KEPT + row // PIECES)
+        first = 32 * PLACE[KEPT + row // PIECES]
         spare = pltpu.roll(in_ref[first:first + CROSS, :], ROWS - 16 * piece, 1)
-        own = in_ref[32 * row:32 * row + CROSS, :]
+        own = in_ref[32 * PLACE[row]:32 * PLACE[row] + CROSS, :]
         out_ref[pl.ds(row, CROSS, stride=KEPT), :] = jnp.where(lane < ROWS, own, spare)
 
 
@@ -232,7 +244,7 @@
             chunk = CHUNKS * group + k
             parts += [
                 rows_ref[CROSS * chunk:CROSS * (chunk + 1), :],
-                in_ref[32 * chunk + 16:32 * chunk + 32, :],
+                in_ref[32 * PLACE[chunk] + 16:32 * PLACE[chunk] + 32, :],
             ]
         system_ref[pl.ds(k, LANES, stride=CHUNKS), :] = jnp.concatenate(parts, axis=0).T
     for copy in copies:
@@ -401,7 +413,9 @@
             )
         ]
     )
-    arrived = lax.all_to_all(packed.reshape(STREAM, 32, LANES), "stream", 0, 0, tiled=True)
+    arrived = lax.all_to_all(
+        packed.reshape(STREAM, 32, LANES), "stream", 0, 0, axis_index_groups=[CORNERS], tiled=True
+    )
     arrived = arrived.reshape(CELLS, LANES)
     faces = pl.pallas_call(
         faces_kernel,

time: 88.8 us -> 89.3 us (level)
    all_to_all x1, blocking collectives: 20.2 us -> 15.6 us  [local(): lax.all_to_all(faces.reshape(5 * CROSS, 1, LANES), 'cross', 0, 0, axis_in...]
    all_to_all x1, blocking collectives: 27.6 us -> 31.6 us  [local(): lax.all_to_all(faces.reshape(CROSS * KEPT // 4, 4, LANES), 'cross', 0, 0,...]
    all_to_all x1, blocking collectives: 12.6 us -> 14.1 us  [local(): lax.all_to_all(results.reshape(STREAM * VARS, 1, LANES), 'stream', 0, 0,...]
where the time goes in v8:
time: 89.3 us; the launch traced here: 89 us
  blocking collectives  82 us (92%)
  Pallas kernels  6.25 us (7%)
    all_to_all x1, blocking collectives, local(): lax.all_to_all(faces.reshape(CROSS * KEPT // 4, 4, LANES), 'cross', 0, 0,...  31.6 us
    all_to_all x1, blocking collectives, local(): lax.all_to_all(packed.reshape(STREAM, 32, LANES), 'stream', 0, 0, axis_in...  20.8 us
    all_to_all x1, blocking collectives, local(): lax.all_to_all(faces.reshape(5 * CROSS, 1, LANES), 'cross', 0, 0, axis_in...  15.6 us
    all_to_all x1, blocking collectives, local(): lax.all_to_all(results.reshape(STREAM * VARS, 1, LANES), 'stream', 0, 0,...  14.1 us
    pallas_call x1, Pallas kernels, local(): pl.pallas_call(solve_kernel, out_shape=[shape(CHUNKS * 4 * VARS, LANES),...  3.11 us

profile of v8, /device:TPU:1, one launch (start us, length us, event | category | flops | bytes accessed | tf_op | source)
XLA Modules:
  0.0 89.0 jit_solution(10060682710282547839)
XLA Ops:
  0.6 1.7 %pack_cells.1 = (f32[1024,128]{1,0:T(8,128)S(1)}, bf16[4,256,256]{2,1,0:T(8,128)(2,1)S(1)}) custom-call(s32[4,16]{1,0:T(4,128)} %bitcast.30, s32[4,16]{1,0:T(4,128)} %bitcast.37, s32[4,16]{1,0:T(4,128)} %bitcast.32, s32[4,16]{1,0:T(4,128)} %bitcast.38, s32[16]{0:T(128)} %live_in.1, f32[5,2,1024]{2,1,0:T(2,128)} %bitcast.36, f32[2,1024]{1,0:T(2,128)} %diagonal_ref.1, ...), custom_call_target="tpu_custom_call" | custom-call | tf_op jit(solution)/shard_map/pack_cells/pallas_call | solution.py:391
  2.3 20.8 %all_to_all.20 = f32[32,32,128]{2,1,0:T(8,128)S(1)} all-to-all(f32[32,32,128]{2,1,0:T(8,128)S(1)} %bitcast.25), channel_id=1, replica_groups={{0,16,480,496,96,112,384,400,32,48,448,464,128,144,352,368,64,80,416,43..., dimensions={0} | all-to-all | bytes 1048576 | tf_op jit(solution)/shard_map/all_to_all | solution.py:416
  23.1 0.1 take_faces.1
  23.3 0.0 copy-start.1
  23.3 0.0 copy-start.2
  23.3 31.6 %all_to_all.21 = f32[112,4,128]{2,1,0:T(4,128)S(1)} all-to-all(f32[112,4,128]{2,1,0:T(4,128)S(1)} %bitcast.24), channel_id=1, replica_groups={{0,15,1,14,2,13,3,12,4,11,5,10,6,9,7,8},{16,31,17,30,18,29,19,28,20,27,..., dimensions={0} | all-to-all | bytes 458752 | tf_op jit(solution)/shard_map/all_to_all | solution.py:428
  54.8 0.0 copy-done.1
  54.8 0.0 copy-done.2
  54.8 3.1 %solve_cells.1 = (f32[160,128]{1,0:T(8,128)S(1)}, f32[80,128]{1,0:T(8,128)S(1)}) custom-call(s32[4,16]{1,0:T(4,128)S(1)} %bitcast.31, s32[4,16]{1,0:T(4,128)S(1)} %bitcast.33, f32[1024,128]{1,0:T(8,128)S(1)} %bitcast.22, f32[448,128]{1,0:T(8,128)S(1)} %bitcast.23), custom_call_target="tpu_custom_call" | custom-call | tf_op jit(solution)/shard_map/solve_cells/pallas_call | solution.py:431
  58.0 15.6 %all_to_all.22 = f32[80,1,128]{2,1,0:T(1,128)S(1)} all-to-all(f32[80,1,128]{2,1,0:T(1,128)S(1)} %bitcast.29), channel_id=1, replica_groups={{0,15,1,14,2,13,3,12,4,11,5,10,6,9,7,8},{16,31,17,30,18,29,19,28,20,27,..., dimensions={0} | all-to-all | bytes 81920 | tf_op jit(solution)/shard_map/all_to_all | solution.py:448
  73.5 0.3 join_faces.1
  73.9 0.0 copy-start
  73.9 14.1 %all_to_all.23 = f32[160,1,128]{2,1,0:T(1,128)S(1)} all-to-all(f32[160,1,128]{2,1,0:T(1,128)S(1)} %bitcast.27), channel_id=1, replica_groups=mesh['stream'=32,'cross'=16] {'stream'}, dimensions={0} | all-to-all | bytes 163840 | tf_op jit(solution)/shard_map/all_to_all | solution.py:458
  88.0 0.0 copy-done
  88.0 1.0 %unpack_cells.1 = (f32[5,2,1024]{2,1,0:T(2,128)}, f32[5,2,1024]{2,1,0:T(2,128)}) custom-call(bf16[4,256,256]{2,1,0:T(8,128)(2,1)S(1)} %get-tuple-element.8.matrix_ref, f32[2,1024]{1,0:T(2,128)S(1)} %copy-done, f32[160,128]{1,0:T(8,128)S(1)} %bitcast.26), custom_call_target="tpu_custom_call" | custom-call | tf_op jit(solution)/shard_map/unpack_cells/pallas_call | solution.py:461
Async XLA Ops:
  23.3 31.6 %copy-start.1 = (s32[16,4]{0,1:T(4,128)S(1)}, s32[16,4]{0,1:T(4,128)}, u32[]{:S(2)}) copy-start(s32[16,4]{0,1:T(4,128)} %param.13) | copy-start | bytes 772
  23.3 31.6 %copy-start.2 = (s32[16,4]{0,1:T(4,128)S(1)}, s32[16,4]{0,1:T(4,128)}, u32[]{:S(2)}) copy-start(s32[16,4]{0,1:T(4,128)} %param.15) | copy-start | bytes 772
  73.9 14.1 %copy-start = (f32[2,1024]{1,0:T(2,128)S(1)}, f32[2,1024]{1,0:T(2,128)}, u32[]{:S(2)}) copy-start(f32[2,1024]{1,0:T(2,128)} %diagonal_ref.1) | copy-start | bytes 24580

commit v9 on v7

--- a/solution.py
+++ b/solution.py
@@ -295,10 +295,13 @@
     fifth = others[0:CROSS]
     for group in range(GROUPS):
         rows = slice(32 * group, 32 * group + CROSS)
-        send_ref[pl.ds(group, CROSS, stride=5), :] = turned[rows]
+        for rank, block in enumerate(ORDER):
+            first = 32 * group + rank
+            send_ref[5 * block + group:5 * block + group + 1, :] = turned[first:first + 1]
         if group:
             fifth = jnp.where(lane_group == group, pltpu.roll(others[rows], 32 * group, 1), fifth)
-    send_ref[pl.ds(4, CROSS, stride=5), :] = fifth
+    for rank, block in enumerate(ORDER):
+        send_ref[5 * block + 4:5 * block + 5, :] = fifth[rank:rank + 1]
 
 
 def regroup(parts):
@@ -318,15 +321,19 @@
     return out
 
 
-def join_kernel(in_ref, face_ref, out_ref, values_ref):
+def join_kernel(in_ref, face_ref, out_ref, values_ref, ranked_ref):
     lane = lax.broadcasted_iota(jnp.int32, (8, LANES), 1)
     returned = (lane & 16) == 0
     blank = jnp.zeros((16, LANES), F32)
-    fifth = face_ref[pl.ds(4, CROSS, stride=5), :]
+    for row in range(5):
+        for rank, block in enumerate(ORDER):
+            first = CROSS * row + rank
+            ranked_ref[first:first + 1, :] = face_ref[5 * block + row:5 * block + row + 1, :]
+    fifth = ranked_ref[4 * CROSS:, :]
     parts = []
     others = []
     for group in range(GROUPS):
-        parts += [face_ref[pl.ds(group, CROSS, stride=5), :], blank]
+        parts += [ranked_ref[CROSS * group:CROSS * (group + 1), :], blank]
         others += [pltpu.roll(fifth, (LANES - 32 * group) % LANES, 1) if group else fifth, blank]
     values_ref[0:LANES, :] = jnp.concatenate(parts, axis=0).T
     values_ref[LANES:2 * LANES, :] = jnp.concatenate(others, axis=0).T
@@ -431,13 +438,15 @@
         compiler_params=PARAMS,
         name="solve_cells",
     )(owner, count, arrived, faces.reshape(CROSS * KEPT, LANES))
-    faces = lax.all_to_all(faces.reshape(5 * CROSS, 1, LANES), "cross", 0, 0, axis_index_groups=[ORDER], tiled=True)
+    faces = lax.all_to_all(faces.reshape(5 * CROSS, 1, LANES), "cross", 0, 0, tiled=True)
     results = pl.pallas_call(
         join_kernel,
         out_shape=shape(STREAM * VARS, LANES),
         in_specs=[VMEM, VMEM],
         out_specs=VMEM,
-        scratch_shapes=[pltpu.VMEM((2 * LANES, LANES), F32)],
+        scratch_shapes=[
+            pltpu.VMEM((2 * LANES, LANES), F32), pltpu.VMEM((5 * CROSS, LANES), F32)
+        ],
         compiler_params=PARAMS,
         name="join_faces",
     )(results, faces.reshape(5 * CROSS, LANES))

time: 88.8 us -> 88.8 us (level)
  no operation moved by 1% of the time
where the time goes in v9:
time: 88.8 us; the launch traced here: 88.5 us
  blocking collectives  81.5 us (92%)
  Pallas kernels  6.26 us (7%)
    all_to_all x1, blocking collectives, local(): lax.all_to_all(faces.reshape(CROSS * KEPT // 4, 4, LANES), 'cross', 0, 0,...  27.6 us
    all_to_all x1, blocking collectives, local(): lax.all_to_all(packed.reshape(STREAM, 32, LANES), 'stream', 0, 0, tiled=T...  21.3 us
    all_to_all x1, blocking collectives, local(): lax.all_to_all(faces.reshape(5 * CROSS, 1, LANES), 'cross', 0, 0, tiled=T...  20.2 us
    all_to_all x1, blocking collectives, local(): lax.all_to_all(results.reshape(STREAM * VARS, 1, LANES), 'stream', 0, 0,...  12.6 us
    pallas_call x1, Pallas kernels, local(): pl.pallas_call(solve_kernel, out_shape=[shape(CHUNKS * 4 * VARS, LANES),...  3.11 us

profile of v9, /device:TPU:1, one launch (start us, length us, event | category | flops | bytes accessed | tf_op | source)
XLA Modules:
  0.0 88.5 jit_solution(17698536481403983971)
XLA Ops:
  0.6 1.7 %pack_cells.1 = (f32[1024,128]{1,0:T(8,128)S(1)}, bf16[4,256,256]{2,1,0:T(8,128)(2,1)S(1)}) custom-call(s32[4,16]{1,0:T(4,128)} %bitcast.30, s32[4,16]{1,0:T(4,128)} %bitcast.37, s32[4,16]{1,0:T(4,128)} %bitcast.32, s32[4,16]{1,0:T(4,128)} %bitcast.38, s32[16]{0:T(128)} %live_in.1, f32[5,2,1024]{2,1,0:T(2,128)} %bitcast.36, f32[2,1024]{1,0:T(2,128)} %diagonal_ref.1, ...), custom_call_target="tpu_custom_call" | custom-call | tf_op jit(solution)/shard_map/pack_cells/pallas_call | solution.py:386
  2.3 21.3 %all_to_all.20 = f32[32,32,128]{2,1,0:T(8,128)S(1)} all-to-all(f32[32,32,128]{2,1,0:T(8,128)S(1)} %bitcast.25), channel_id=1, replica_groups=mesh['stream'=32,'cross'=16] {'stream'}, dimensions={0} | all-to-all | bytes 1048576 | tf_op jit(solution)/shard_map/all_to_all | solution.py:411
  23.6 0.1 take_faces.1
  23.7 0.0 copy-start.1
  23.7 0.0 copy-start.2
  23.7 27.6 %all_to_all.21 = f32[112,4,128]{2,1,0:T(4,128)S(1)} all-to-all(f32[112,4,128]{2,1,0:T(4,128)S(1)} %bitcast.24), channel_id=1, replica_groups={{0,2,4,6,8,10,12,14,15,13,11,9,7,5,3,1},{16,18,20,22,24,26,28,30,31,29,..., dimensions={0} | all-to-all | bytes 458752 | tf_op jit(solution)/shard_map/all_to_all | solution.py:421
  51.3 0.0 copy-done.1
  51.3 0.0 copy-done.2
  51.3 3.1 %solve_cells.1 = (f32[160,128]{1,0:T(8,128)S(1)}, f32[80,128]{1,0:T(8,128)S(1)}) custom-call(s32[4,16]{1,0:T(4,128)S(1)} %bitcast.31, s32[4,16]{1,0:T(4,128)S(1)} %bitcast.33, f32[1024,128]{1,0:T(8,128)S(1)} %bitcast.22, f32[448,128]{1,0:T(8,128)S(1)} %bitcast.23), custom_call_target="tpu_custom_call" | custom-call | tf_op jit(solution)/shard_map/solve_cells/pallas_call | solution.py:424
  54.4 20.2 %all_to_all.22 = f32[80,1,128]{2,1,0:T(1,128)S(1)} all-to-all(f32[80,1,128]{2,1,0:T(1,128)S(1)} %bitcast.29), channel_id=1, replica_groups=mesh['stream'=32,'cross'=16] {'cross'}, dimensions={0} | all-to-all | bytes 81920 | tf_op jit(solution)/shard_map/all_to_all | solution.py:441
  74.6 0.3 join_faces.1
  74.9 0.0 copy-start
  74.9 12.6 %all_to_all.23 = f32[160,1,128]{2,1,0:T(1,128)S(1)} all-to-all(f32[160,1,128]{2,1,0:T(1,128)S(1)} %bitcast.27), channel_id=1, replica_groups=mesh['stream'=32,'cross'=16] {'stream'}, dimensions={0} | all-to-all | bytes 163840 | tf_op jit(solution)/shard_map/all_to_all | solution.py:453
  87.5 0.0 copy-done
  87.5 1.0 %unpack_cells.1 = (f32[5,2,1024]{2,1,0:T(2,128)}, f32[5,2,1024]{2,1,0:T(2,128)}) custom-call(bf16[4,256,256]{2,1,0:T(8,128)(2,1)S(1)} %get-tuple-element.8.matrix_ref, f32[2,1024]{1,0:T(2,128)S(1)} %copy-done, f32[160,128]{1,0:T(8,128)S(1)} %bitcast.26), custom_call_target="tpu_custom_call" | custom-call | tf_op jit(solution)/shard_map/unpack_cells/pallas_call | solution.py:456
Async XLA Ops:
  23.7 27.6 %copy-start.1 = (s32[16,4]{0,1:T(4,128)S(1)}, s32[16,4]{0,1:T(4,128)}, u32[]{:S(2)}) copy-start(s32[16,4]{0,1:T(4,128)} %param.13) | copy-start | bytes 772
  23.7 27.6 %copy-start.2 = (s32[16,4]{0,1:T(4,128)S(1)}, s32[16,4]{0,1:T(4,128)}, u32[]{:S(2)}) copy-start(s32[16,4]{0,1:T(4,128)} %param.15) | copy-start | bytes 772
  74.9 12.6 %copy-start = (f32[2,1024]{1,0:T(2,128)S(1)}, f32[2,1024]{1,0:T(2,128)}, u32[]{:S(2)}) copy-start(f32[2,1024]{1,0:T(2,128)} %diagonal_ref.1) | copy-start | bytes 24580

commit v10 on v5

--- a/solution.py
+++ b/solution.py
@@ -83,26 +83,27 @@
     copies = copy_in(
         [
             (owner_in, owner_ref), (start_in, start_ref), (count_in, count_ref),
-            (flip_in, flip_ref), (live_in, live_ref), (rhs_in, rhs_ref),
-            (diagonal_in, diagonal_ref), (lower_in, lower_ref), (upper_in, upper_ref),
+            (flip_in, flip_ref), (lower_in, lower_ref), (upper_in, upper_ref),
+            (live_in, live_ref), (rhs_in, rhs_ref), (diagonal_in, diagonal_ref),
         ],
         sems,
     )
     own = lax.axis_index("cross")
     rows_ref[pl.ds(ROWS, LANES - ROWS), :] = jnp.zeros((LANES - ROWS, CELLS), F32)
-    for copy in copies[:5]:
+    for copy in copies[:4]:
         copy.wait()
     for link in range(LINKS):
         matrix_ref[link] = onehot(slots_of(own, link, owner_ref, start_ref, count_ref, flip_ref))
-    for copy in copies[5:]:
+    for copy, first, ref in ((copies[4], LOWER, lower_ref), (copies[5], UPPER, upper_ref)):
+        copy.wait()
+        for a in range(VARS):
+            for b in range(VARS):
+                rows_ref[pl.ds(2 * (first + VARS * a + b), 2), :] = ref[a, b]
+    for copy in copies[6:]:
         copy.wait()
     cell = lax.broadcasted_iota(jnp.int32, (PLANES, CELLS), 1)
     live = cell < live_ref[own]
     for a in range(VARS):
-        for b in range(VARS):
-            at = VARS * a + b
-            rows_ref[pl.ds(2 * (LOWER + at), 2), :] = lower_ref[a, b]
-            rows_ref[pl.ds(2 * (UPPER + at), 2), :] = upper_ref[a, b]
         source = jnp.where(live, rhs_ref[a], 0.0) / diagonal_ref[...]
         rows_ref[pl.ds(2 * (SOURCE + a), 2), :] = source
     for link in range(LINKS):

time: 89 us -> 89 us (level)
  no operation moved by 1% of the time
where the time goes in v10:
time: 89 us; the launch traced here: 88.7 us
  blocking collectives  81.8 us (92%)
  Pallas kernels  6.14 us (7%)
    all_to_all x1, blocking collectives, local(): lax.all_to_all(faces.reshape(CROSS * KEPT // 4, 4, LANES), 'cross', 0, 0,...  27.4 us
    all_to_all x1, blocking collectives, local(): lax.all_to_all(packed.reshape(STREAM, 32, LANES), 'stream', 0, 0, tiled=T...  21.3 us
    all_to_all x1, blocking collectives, local(): lax.all_to_all(faces.reshape(5 * CROSS, 1, LANES), 'cross', 0, 0, tiled=T...  20.3 us
    all_to_all x1, blocking collectives, local(): returned = lax.all_to_all(results, 'stream', 0, 0, tiled=True)  12.8 us
    pallas_call x1, Pallas kernels, local(): pl.pallas_call(solve_kernel, out_shape=[shape(CHUNKS * 32, LANES), shape(...  3.01 us

profile of v10, /device:TPU:1, one launch (start us, length us, event | category | flops | bytes accessed | tf_op | source)
XLA Modules:
  0.0 88.7 jit_solution(14552339536884261733)
XLA Ops:
  0.6 1.7 %pack_cells.1 = (f32[1024,128]{1,0:T(8,128)S(1)}, bf16[4,256,256]{2,1,0:T(8,128)(2,1)S(1)}) custom-call(s32[4,16]{1,0:T(4,128)} %bitcast.24, s32[4,16]{1,0:T(4,128)} %bitcast.31, s32[4,16]{1,0:T(4,128)} %bitcast.26, s32[4,16]{1,0:T(4,128)} %bitcast.32, s32[16]{0:T(128)} %live_in.1, f32[5,2,1024]{2,1,0:T(2,128)} %bitcast.30, f32[2,1024]{1,0:T(2,128)} %diagonal_ref.1, ...), custom_call_target="tpu_custom_call" | custom-call | tf_op jit(solution)/shard_map/pack_cells/pallas_call | solution.py:366
  2.3 21.3 %all_to_all.20 = f32[32,32,128]{2,1,0:T(8,128)S(1)} all-to-all(f32[32,32,128]{2,1,0:T(8,128)S(1)} %bitcast.21), channel_id=1, replica_groups=mesh['stream'=32,'cross'=16] {'stream'}, dimensions={0} | all-to-all | bytes 1048576 | tf_op jit(solution)/shard_map/all_to_all | solution.py:391
  23.5 0.1 take_faces.1
  23.7 0.0 copy-start.1
  23.7 0.0 copy-start.2
  23.7 27.4 %all_to_all.21 = f32[112,4,128]{2,1,0:T(4,128)S(1)} all-to-all(f32[112,4,128]{2,1,0:T(4,128)S(1)} %bitcast.20), channel_id=1, replica_groups=mesh['stream'=32,'cross'=16] {'cross'}, dimensions={0} | all-to-all | bytes 458752 | tf_op jit(solution)/shard_map/all_to_all | solution.py:401
  51.1 0.0 copy-done.1
  51.1 0.0 copy-done.2
  51.1 3.0 %solve_cells.1 = (f32[256,128]{1,0:T(8,128)S(1)}, f32[80,128]{1,0:T(8,128)S(1)}) custom-call(s32[4,16]{1,0:T(4,128)S(1)} %bitcast.25, s32[4,16]{1,0:T(4,128)S(1)} %bitcast.27, f32[1024,128]{1,0:T(8,128)S(1)} %bitcast.18, f32[448,128]{1,0:T(8,128)S(1)} %bitcast.19), custom_call_target="tpu_custom_call" | custom-call | tf_op jit(solution)/shard_map/solve_cells/pallas_call | solution.py:404
  54.1 20.3 %all_to_all.22 = f32[80,1,128]{2,1,0:T(1,128)S(1)} all-to-all(f32[80,1,128]{2,1,0:T(1,128)S(1)} %bitcast.23), channel_id=1, replica_groups=mesh['stream'=32,'cross'=16] {'cross'}, dimensions={0} | all-to-all | bytes 81920 | tf_op jit(solution)/shard_map/all_to_all | solution.py:420
  74.5 0.4 join_faces.1
  74.8 0.0 copy-start
  74.8 12.8 %all_to_all.23.in_ref = f32[32,8,128]{2,1,0:T(8,128)S(1)} all-to-all(f32[32,8,128]{2,1,0:T(8,128)S(1)} %join_faces.1), channel_id=1, replica_groups=mesh['stream'=32,'cross'=16] {'stream'}, dimensions={0} | all-to-all | bytes 262144 | tf_op jit(solution)/shard_map/all_to_all | solution.py:430
  87.7 0.0 copy-done
  87.7 1.0 %unpack_cells.1 = (f32[5,2,1024]{2,1,0:T(2,128)}, f32[5,2,1024]{2,1,0:T(2,128)}) custom-call(bf16[4,256,256]{2,1,0:T(8,128)(2,1)S(1)} %get-tuple-element.8.matrix_ref, f32[2,1024]{1,0:T(2,128)S(1)} %copy-done, f32[32,8,128]{2,1,0:T(8,128)S(1)} %all_to_all.23.in_ref), custom_call_target="tpu_custom_call" | custom-call | tf_op jit(solution)/shard_map/unpack_cells/pallas_call | solution.py:431
Async XLA Ops:
  23.7 27.4 %copy-start.1 = (s32[16,4]{0,1:T(4,128)S(1)}, s32[16,4]{0,1:T(4,128)}, u32[]{:S(2)}) copy-start(s32[16,4]{0,1:T(4,128)} %param.13) | copy-start | bytes 772
  23.7 27.4 %copy-start.2 = (s32[16,4]{0,1:T(4,128)S(1)}, s32[16,4]{0,1:T(4,128)}, u32[]{:S(2)}) copy-start(s32[16,4]{0,1:T(4,128)} %param.15) | copy-start | bytes 772
  74.8 12.8 %copy-start = (f32[2,1024]{1,0:T(2,128)S(1)}, f32[2,1024]{1,0:T(2,128)}, u32[]{:S(2)}) copy-start(f32[2,1024]{1,0:T(2,128)} %diagonal_ref.1) | copy-start | bytes 24580

commit v11 on v5

--- a/solution.py
+++ b/solution.py
@@ -142,12 +142,18 @@
             out_ref[VARS * a + c] = x
 
 
-def relay(matrix_ref, offset, offset_ref, state_ref, up):
-    for a in range(VARS):
-        offset_ref[a] = offset[a]
+def relay(matrix_ref, pair_ref, offset, offset_ref, state_ref, up):
+    back = 1 if up else CHUNKS - 1
+    matrix = [[matrix_ref[VARS * a + b] for b in range(VARS)] for a in range(VARS)]
+
+    def passed(x, first=None):
+        return total([[matrix[a][b] * x[b] for b in range(VARS)] for a in range(VARS)], first)
+
+    for a, x in enumerate(passed([pltpu.roll(x, back, 0) for x in offset], offset)):
+        offset_ref[a] = x
     state = [jnp.zeros((1, LANES), F32) for _ in range(VARS)]
     groups = range(GROUPS) if up else range(GROUPS - 1, -1, -1)
-    chunks = range(CHUNKS) if up else range(CHUNKS - 1, -1, -1)
+    chunks = range(0, CHUNKS, 2) if up else range(CHUNKS - 1, -1, -2)
     for group in groups:
         if group != groups[0]:
             state = [pltpu.roll(x, 32 if up else 96, 1) for x in state]
@@ -155,9 +161,10 @@
             row = slice(k, k + 1)
             for a in range(VARS):
                 state_ref[group, a, row, :] = state[a]
+            row = slice(k + 1, k + 2) if up else slice(k - 1, k)
             state = total(
                 [
-                    [matrix_ref[VARS * a + b, row, :] * state[b] for b in range(VARS)]
+                    [pair_ref[VARS * a + b, row, :] * state[b] for b in range(VARS)]
                     for a in range(VARS)
                 ],
                 [offset_ref[a, row, :] for a in range(VARS)],
@@ -169,7 +176,19 @@
         for group in range(GROUPS - 1):
             x = jnp.where(lane == group, state_ref[group, a], x)
         out.append(x)
-    return out
+    row = lax.broadcasted_iota(jnp.int32, (CHUNKS, LANES), 0) & 1
+    inner = [pltpu.roll(x, back, 0) for x in passed(out, offset)]
+    return [jnp.where(row == (0 if up else 1), x, y) for x, y in zip(out, inner)]
+
+
+def pair(matrix_ref, pair_ref, up):
+    for c in range(VARS):
+        column = [
+            pltpu.roll(matrix_ref[VARS * b + c], 1 if up else CHUNKS - 1, 0) for b in range(VARS)
+        ]
+        for a in range(VARS):
+            t = [matrix_ref[VARS * a + b] * column[b] for b in range(VARS)]
+            pair_ref[VARS * a + c] = total([t])[0]
 
 
 def plus(x, y):
@@ -215,7 +234,7 @@
 
 def solve_kernel(
     owner_in, count_in, in_ref, face_ref, out_ref, send_ref,
-    owner_ref, count_ref, system_ref, lower_ref, upper_ref, offset_ref, state_ref, values_ref, sems,
+    owner_ref, count_ref, system_ref, lower_ref, upper_ref, lower_pair, upper_pair, offset_ref, state_ref, values_ref, sems,
 ):
     copies = copy_in([(owner_in, owner_ref), (count_in, count_ref)], sems)
     values_ref[160:, :] = jnp.zeros((96, LANES), F32)
@@ -232,10 +251,12 @@
     upper = functools.partial(apply, system_ref, UPPER)
     compose(system_ref, LOWER, 1, 0, lower_ref)
     compose(system_ref, UPPER, 0, 1, upper_ref)
+    pair(lower_ref, lower_pair, True)
+    pair(upper_ref, upper_pair, False)
 
     def upper_sweep(lowered):
         offset = upper(0, lowered[1], lowered[0])
-        after = relay(upper_ref, offset, offset_ref, state_ref, False)
+        after = relay(upper_ref, upper_pair, offset, offset_ref, state_ref, False)
         coupled_1 = upper(1, after)
         delta_1 = plus(lowered[1], coupled_1)
         coupled_0 = upper(0, delta_1)
@@ -247,7 +268,7 @@
         return [rows[:VARS], rows[VARS:]]
 
     source = [[entry(system_ref, SOURCE + a, p) for a in range(VARS)] for p in range(PLANES)]
-    before = relay(lower_ref, lower(1, source[0], source[1]), offset_ref, state_ref, True)
+    before = relay(lower_ref, lower_pair, lower(1, source[0], source[1]), offset_ref, state_ref, True)
     lowered_0 = lower(0, before, source[0])
     lowered_1 = lower(1, lowered_0, source[1])
     coupled, first = upper_sweep([lowered_0, lowered_1])
@@ -255,7 +276,7 @@
     faces = faces_of(first)
     joint_0 = plus(faces[0], coupled[0])
     joint_1 = plus(faces[1], coupled[1])
-    before = relay(lower_ref, lower(1, joint_0, joint_1), offset_ref, state_ref, True)
+    before = relay(lower_ref, lower_pair, lower(1, joint_0, joint_1), offset_ref, state_ref, True)
     along = lower(0, before)
     lowered_1 = lower(1, plus(joint_0, along), faces[1])
     coupled, second = upper_sweep([plus(faces[0], along), lowered_1])
@@ -407,7 +428,7 @@
         out_specs=[VMEM, VMEM],
         scratch_shapes=[TABLE] * 2
         + [
-            pltpu.VMEM((CHUNKS * LANES, LANES), F32), composed, composed,
+            pltpu.VMEM((CHUNKS * LANES, LANES), F32), composed, composed, composed, composed,
             pltpu.VMEM((VARS, CHUNKS, LANES), F32),
             pltpu.VMEM((GROUPS, VARS, CHUNKS, LANES), F32),
             pltpu.VMEM((2 * LANES, LANES), F32),

time: 89 us -> 88.7 us (level)
  no operation moved by 1% of the time
where the time goes in v11:
time: 88.7 us; the launch traced here: 88.4 us
  blocking collectives  81.8 us (92%)
  Pallas kernels  5.87 us (7%)
    all_to_all x1, blocking collectives, local(): lax.all_to_all(faces.reshape(CROSS * KEPT // 4, 4, LANES), 'cross', 0, 0,...  27.4 us
    all_to_all x1, blocking collectives, local(): lax.all_to_all(packed.reshape(STREAM, 32, LANES), 'stream', 0, 0, tiled=T...  21.3 us
    all_to_all x1, blocking collectives, local(): lax.all_to_all(faces.reshape(5 * CROSS, 1, LANES), 'cross', 0, 0, tiled=T...  20.3 us
    all_to_all x1, blocking collectives, local(): returned = lax.all_to_all(results, 'stream', 0, 0, tiled=True)  12.8 us
    pallas_call x1, Pallas kernels, local(): pl.pallas_call(solve_kernel, out_shape=[shape(CHUNKS * 32, LANES), shape(...  2.72 us

profile of v11, /device:TPU:1, one launch (start us, length us, event | category | flops | bytes accessed | tf_op | source)
XLA Modules:
  0.0 88.4 jit_solution(3266295693538562204)
XLA Ops:
  0.6 1.7 %pack_cells.1 = (f32[1024,128]{1,0:T(8,128)S(1)}, bf16[4,256,256]{2,1,0:T(8,128)(2,1)S(1)}) custom-call(s32[4,16]{1,0:T(4,128)} %bitcast.24, s32[4,16]{1,0:T(4,128)} %bitcast.31, s32[4,16]{1,0:T(4,128)} %bitcast.26, s32[4,16]{1,0:T(4,128)} %bitcast.32, s32[16]{0:T(128)} %live_in.1, f32[5,2,1024]{2,1,0:T(2,128)} %bitcast.30, f32[2,1024]{1,0:T(2,128)} %diagonal_ref.1, ...), custom_call_target="tpu_custom_call" | custom-call | tf_op jit(solution)/shard_map/pack_cells/pallas_call | solution.py:386
  2.3 21.3 %all_to_all.20 = f32[32,32,128]{2,1,0:T(8,128)S(1)} all-to-all(f32[32,32,128]{2,1,0:T(8,128)S(1)} %bitcast.21), channel_id=1, replica_groups=mesh['stream'=32,'cross'=16] {'stream'}, dimensions={0} | all-to-all | bytes 1048576 | tf_op jit(solution)/shard_map/all_to_all | solution.py:411
  23.6 0.1 take_faces.1
  23.7 0.0 copy-start.1
  23.7 0.0 copy-start.2
  23.7 27.4 %all_to_all.21 = f32[112,4,128]{2,1,0:T(4,128)S(1)} all-to-all(f32[112,4,128]{2,1,0:T(4,128)S(1)} %bitcast.20), channel_id=1, replica_groups=mesh['stream'=32,'cross'=16] {'cross'}, dimensions={0} | all-to-all | bytes 458752 | tf_op jit(solution)/shard_map/all_to_all | solution.py:421
  51.1 0.0 copy-done.1
  51.1 0.0 copy-done.2
  51.1 2.7 %solve_cells.1 = (f32[256,128]{1,0:T(8,128)S(1)}, f32[80,128]{1,0:T(8,128)S(1)}) custom-call(s32[4,16]{1,0:T(4,128)S(1)} %bitcast.25, s32[4,16]{1,0:T(4,128)S(1)} %bitcast.27, f32[1024,128]{1,0:T(8,128)S(1)} %bitcast.18, f32[448,128]{1,0:T(8,128)S(1)} %bitcast.19), custom_call_target="tpu_custom_call" | custom-call | tf_op jit(solution)/shard_map/solve_cells/pallas_call | solution.py:424
  53.9 20.3 %all_to_all.22 = f32[80,1,128]{2,1,0:T(1,128)S(1)} all-to-all(f32[80,1,128]{2,1,0:T(1,128)S(1)} %bitcast.23), channel_id=1, replica_groups=mesh['stream'=32,'cross'=16] {'cross'}, dimensions={0} | all-to-all | bytes 81920 | tf_op jit(solution)/shard_map/all_to_all | solution.py:440
  74.2 0.4 join_faces.1
  74.6 0.0 copy-start
  74.6 12.8 %all_to_all.23.in_ref = f32[32,8,128]{2,1,0:T(8,128)S(1)} all-to-all(f32[32,8,128]{2,1,0:T(8,128)S(1)} %join_faces.1), channel_id=1, replica_groups=mesh['stream'=32,'cross'=16] {'stream'}, dimensions={0} | all-to-all | bytes 262144 | tf_op jit(solution)/shard_map/all_to_all | solution.py:450
  87.4 0.0 copy-done
  87.4 1.0 %unpack_cells.1 = (f32[5,2,1024]{2,1,0:T(2,128)}, f32[5,2,1024]{2,1,0:T(2,128)}) custom-call(bf16[4,256,256]{2,1,0:T(8,128)(2,1)S(1)} %get-tuple-element.8.matrix_ref, f32[2,1024]{1,0:T(2,128)S(1)} %copy-done, f32[32,8,128]{2,1,0:T(8,128)S(1)} %all_to_all.23.in_ref), custom_call_target="tpu_custom_call" | custom-call | tf_op jit(solution)/shard_map/unpack_cells/pallas_call | solution.py:451
Async XLA Ops:
  23.7 27.4 %copy-start.1 = (s32[16,4]{0,1:T(4,128)S(1)}, s32[16,4]{0,1:T(4,128)}, u32[]{:S(2)}) copy-start(s32[16,4]{0,1:T(4,128)} %param.13) | copy-start | bytes 772
  23.7 27.4 %copy-start.2 = (s32[16,4]{0,1:T(4,128)S(1)}, s32[16,4]{0,1:T(4,128)}, u32[]{:S(2)}) copy-start(s32[16,4]{0,1:T(4,128)} %param.15) | copy-start | bytes 772
  74.6 12.8 %copy-start = (f32[2,1024]{1,0:T(2,128)S(1)}, f32[2,1024]{1,0:T(2,128)}, u32[]{:S(2)}) copy-start(f32[2,1024]{1,0:T(2,128)} %diagonal_ref.1) | copy-start | bytes 24580
